TPU v7x, 32 devices: a whole 2x2x4 slice. The times are simulated.
32 devices in a mesh: gx: 4 (over y, x), gy: 8 (over z, core).
Axes of the slice: x: 2, y: 2, z: 4, core: 2. Of those that a mesh axis runs over, the one named last changes fastest.
Arguments:
- u_face: float32 [8, 2048, 2048], P(None, 'gy', 'gx'), may hold values from -6 to 6
- v_face: float32 [8, 2048, 2048], P(None, 'gy', 'gx'), may hold values from -6 to 6
- w_face: float32 [8, 2048, 2048], P(None, 'gy', 'gx'), may hold values from -6 to 6
- theta_field: float32 [8, 2048, 2048], P(None, 'gy', 'gx'), may hold values from -6 to 6
- density: float32 [8], replicated, may hold values from 0.3 to 1.5
- thickness: float32 [8], replicated, may hold values from 4 to 32
Outputs:
- u_new: float32 [8, 2048, 2048], P(None, 'gy', 'gx')
- v_new: float32 [8, 2048, 2048], P(None, 'gy', 'gx')
- w_new: float32 [8, 2048, 2048], P(None, 'gy', 'gx')
- theta_new: float32 [8, 2048, 2048], P(None, 'gy', 'gx')
- pressure: float32 [8, 2048, 2048], P(None, 'gy', 'gx')
All inputs are finite; a program needn't handle non-finite values.
Results may differ from a plain program's by a relative error of at most 0.0003.
Values sent between devices are 32-bit elements; how exact they have to be, the bound alone decides.
No kernel may reach another device: no remote copies, remote signals or barrier semaphores. Data moves between devices by JAX's collectives and lax.ppermute only.
A program may use at most 192 MiB of HBM per device.

v0:
```python
import math

import jax
import jax.numpy as jnp
from jax import lax
from jax.sharding import PartitionSpec as P

time_step = 0.2
buoyancy_gain = 1.0


def from_behind(value, axis, steps):
    count = lax.axis_size(axis)
    pairs = [(source, (source + steps) % count) for source in range(count)]
    return lax.ppermute(value, axis, pairs)


def extended(value, sides, width):
    for axis, dim in sides:
        size, length = (lax.axis_size(axis), value.shape[dim])
        up = [(i, (i + 1) % size) for i in range(size)]
        down = [(j, i) for i, j in up]
        last = lax.slice_in_dim(value, length - width, length, axis=dim)
        first = lax.slice_in_dim(value, 0, width, axis=dim)
        before = lax.ppermute(last, axis, up)
        after = lax.ppermute(first, axis, down)
        value = jnp.concatenate([before, value, after], axis=dim)
    return value


def lift_level(field):
    return jnp.concatenate([field[1:], field[-1:]], axis=0)


def upwind_flux(q_m2, q_m1, q_zero, q_p1, q_p2, q_p3, velocity):
    centred = velocity * (37.0 * (q_zero + q_p1) - 8.0 * (q_m1 + q_p2) + (q_m2 + q_p3)) / 60.0
    damped = (
        jnp.abs(velocity) * (10.0 * (q_p1 - q_zero) - 5.0 * (q_p2 - q_m1) + (q_p3 - q_m2)) / 60.0
    )
    return centred - damped


def vertical_tend(tracer, velocity, rho_face, rho_level, spacing):
    levels = tracer.shape[0]
    padded = jnp.pad(tracer, ((2, 3), (0, 0), (0, 0)), mode="edge")
    parts = [padded[2 + offset : 2 + offset + levels] for offset in range(-2, 4)]
    flux_z = upwind_flux(*parts, velocity) * rho_face[:, None, None]
    below = jnp.concatenate([jnp.zeros_like(flux_z[:1]), flux_z[:-1]], axis=0)
    return -(flux_z - below) / (rho_level * spacing)[:, None, None]


def horizontal_local(tracer_rim, u_rim, v_rim, rows_y, cols_x):
    row_band = tracer_rim[:, 3 : 3 + rows_y, :]
    parts_x = [row_band[:, :, 2 + offset : 3 + offset + cols_x] for offset in range(-2, 4)]
    flux_x = upwind_flux(*parts_x, u_rim[:, 3 : 3 + rows_y, 2 : 3 + cols_x])
    col_band = tracer_rim[:, :, 3 : 3 + cols_x]
    parts_y = [col_band[:, 2 + offset : 3 + offset + rows_y, :] for offset in range(-2, 4)]
    flux_y = upwind_flux(*parts_y, v_rim[:, 2 : 3 + rows_y, 3 : 3 + cols_x])
    return -(flux_x[:, :, 1:] - flux_x[:, :, :-1]) - (flux_y[:, 1:, :] - flux_y[:, :-1, :])


def twiddle(rows, cols, count):
    row_idx = jnp.arange(rows, dtype=jnp.int32)
    col_idx = jnp.arange(cols, dtype=jnp.int32)
    product_mod = row_idx[:, None] * col_idx[None, :] % count
    angles = product_mod.astype(jnp.float32) * (2.0 * math.pi / count)
    return (jnp.cos(angles), jnp.sin(angles))


def hartley_axis(field, axis):
    shape = field.shape
    count = shape[axis]
    before = 1
    for extent in shape[:axis]:
        before = before * extent
    after = 1
    for extent in shape[axis + 1 :]:
        after = after * extent
    bits = count.bit_length() - 1
    inner_len = 2 ** (bits // 2)
    outer_len = count // inner_len
    tail = "b" if after > 1 else ""
    if after > 1:
        shaped = field.reshape(before, outer_len, inner_len, after)
    else:
        shaped = field.reshape(before, outer_len, inner_len)
    cos_q, sin_q = twiddle(outer_len, outer_len, outer_len)
    cos_t, sin_t = twiddle(outer_len, inner_len, count)
    cos_p, sin_p = twiddle(inner_len, inner_len, inner_len)
    if after > 1:
        cos_t = cos_t[None, :, :, None]
        sin_t = sin_t[None, :, :, None]
    else:
        cos_t = cos_t[None, :, :]
        sin_t = sin_t[None, :, :]
    high = lax.Precision.HIGHEST
    first_form = "aqp" + tail + ",mq->amp" + tail
    real_part = jnp.einsum(first_form, shaped, cos_q, precision=high)
    imag_part = -jnp.einsum(first_form, shaped, sin_q, precision=high)
    twisted_re = real_part * cos_t + imag_part * sin_t
    twisted_im = imag_part * cos_t - real_part * sin_t
    second_form = "amp" + tail + ",np->anm" + tail
    result = jnp.einsum(second_form, twisted_re, cos_p + sin_p, precision=high)
    result = result + jnp.einsum(second_form, twisted_im, sin_p - cos_p, precision=high)
    return result.reshape(shape)


def eigen_line(indices, count):
    return -4.0 * jnp.sin(math.pi * indices.astype(jnp.float32) / count) ** 2


def tridiag_solve(lower_coef, upper_coef, eigen_sum, source_term):
    levels = source_term.shape[0]
    shape_b = (levels,) + (1,) * (source_term.ndim - 1)
    low_b = lower_coef.reshape(shape_b)
    high_b = upper_coef.reshape(shape_b)
    ratios = []
    partial_sols = []
    for level in range(levels):
        pivots = eigen_sum - low_b[level] - high_b[level]
        numerator = source_term[level]
        if level > 0:
            pivots = pivots - low_b[level] * ratios[-1]
            numerator = numerator - low_b[level] * partial_sols[-1]
        ratios.append(high_b[level] / pivots)
        partial_sols.append(numerator / pivots)
    solved_levels = [partial_sols[-1]]
    for level in range(levels - 2, -1, -1):
        solved_levels.append(partial_sols[level] - ratios[level] * solved_levels[-1])
    return jnp.stack(solved_levels[::-1], axis=0)


def shift_gradient(pressure):
    east_cells = from_behind(pressure[:, :, :1], "gx", -1)
    north_cells = from_behind(pressure[:, :1, :], "gy", -1)
    grad_x = jnp.concatenate([pressure[:, :, 1:], east_cells], axis=2) - pressure
    grad_y = jnp.concatenate([pressure[:, 1:, :], north_cells], axis=1) - pressure
    return (grad_x, grad_y)


def per_device(u_face, v_face, w_face, theta_field, density, thickness):
    groups_x = lax.axis_size("gx")
    groups_y = lax.axis_size("gy")
    levels, rows_y, cols_x = theta_field.shape
    cells_x = cols_x * groups_x
    cells_y = rows_y * groups_y
    theta_rim, w_rim, u_rim, v_rim = (
        extended(theta_field, (("gx", 2), ("gy", 1)), 3),
        extended(w_face, (("gx", 2), ("gy", 1)), 3),
        extended(u_face, (("gx", 2), ("gy", 1)), 3),
        extended(v_face, (("gx", 2), ("gy", 1)), 3),
    )
    face_density = (density + lift_level(density)) / 2.0
    face_spacing = (thickness + lift_level(thickness)) / 2.0
    adv_theta = horizontal_local(theta_rim, u_rim, v_rim, rows_y, cols_x) + vertical_tend(
        theta_field, w_face, face_density, density, thickness
    )
    u_level = (u_rim + lift_level(u_rim)) / 2.0
    v_level = (v_rim + lift_level(v_rim)) / 2.0
    w_level = (w_face + lift_level(w_face)) / 2.0
    adv_w = horizontal_local(w_rim, u_level, v_level, rows_y, cols_x) + vertical_tend(
        w_face, w_level, lift_level(density), face_density, face_spacing
    )
    theta_new = theta_field + time_step * adv_theta
    w_star = w_face + time_step * (
        adv_w + buoyancy_gain * (theta_field + lift_level(theta_field)) / 2.0
    )
    mass_flux = face_density[:, None, None] * w_star
    mass_below = jnp.concatenate([jnp.zeros_like(mass_flux[:1]), mass_flux[:-1]], axis=0)
    divergence = (
        u_face
        - u_rim[:, 3 : 3 + rows_y, 2 : 2 + cols_x]
        + (v_face - v_rim[:, 2 : 2 + rows_y, 3 : 3 + cols_x])
    )
    divergence = divergence + (mass_flux - mass_below) / (density * thickness)[:, None, None]
    source_term = divergence / time_step
    lower_coef = jnp.concatenate(
        [
            jnp.zeros((1,), jnp.float32),
            face_density[:-1] / (density[1:] * thickness[1:] * face_spacing[:-1]),
        ]
    )
    upper_coef = face_density / (density * thickness * face_spacing)

    def forward_x(blocks):
        return hartley_axis(blocks, blocks.ndim - 1)

    def forward_y(blocks):
        return hartley_axis(blocks, 1)

    width_kx = cells_x // groups_y
    eig_x = eigen_line(
        lax.axis_index("gy") * width_kx + jnp.arange(width_kx, dtype=jnp.int32), cells_x
    )
    lines = forward_x(lax.all_to_all(source_term, "gx", split_axis=0, concat_axis=2, tiled=True))
    spectra = forward_y(lax.all_to_all(lines, "gy", split_axis=2, concat_axis=1, tiled=True))
    columns = lax.all_to_all(spectra, "gx", split_axis=1, concat_axis=0, tiled=True)
    width_ky = cells_y // groups_x
    eig_y = eigen_line(
        lax.axis_index("gx") * width_ky + jnp.arange(width_ky, dtype=jnp.int32), cells_y
    )
    eigen_sum = (eig_y[:, None] + eig_x[None, :]).reshape(-1)
    solution = tridiag_solve(
        lower_coef, upper_coef, eigen_sum, columns.reshape(levels, -1)
    ).reshape(columns.shape)
    solved = lax.all_to_all(solution, "gx", split_axis=0, concat_axis=1, tiled=True)
    back_y = forward_y(solved) / cells_y
    rows_x = (
        forward_x(lax.all_to_all(back_y, "gy", split_axis=1, concat_axis=2, tiled=True)) / cells_x
    )
    pressure = lax.all_to_all(rows_x, "gx", split_axis=2, concat_axis=0, tiled=True)
    grad_x, grad_y = shift_gradient(pressure)
    u_new = u_face - time_step * grad_x
    v_new = v_face - time_step * grad_y
    above = jnp.concatenate([pressure[1:], jnp.zeros_like(pressure[:1])], axis=0)
    w_new = w_star - time_step * (above - pressure) / face_spacing[:, None, None]
    return (u_new, v_new, w_new, theta_new, pressure)


def solution(mesh):
    return jax.shard_map(
        per_device,
        mesh=mesh,
        in_specs=(
            P(None, "gy", "gx"),
            P(None, "gy", "gx"),
            P(None, "gy", "gx"),
            P(None, "gy", "gx"),
            P(),
            P(),
        ),
        out_specs=(
            P(None, "gy", "gx"),
            P(None, "gy", "gx"),
            P(None, "gy", "gx"),
            P(None, "gy", "gx"),
            P(None, "gy", "gx"),
        ),
        check_vma=False,
    )
```

profile of v0, /device:TPU:0, one launch (start us, length us, event | category | flops | bytes accessed | tf_op | source)
XLA Modules:
  0.0 926.5 jit_solution(1192755359572399721)
XLA Ops:
  66.1 22.9 %multiply_subtract_fusion = f32[8,256,513]{2,1,0:T(8,128)} fusion(f32[8,256,512]{2,1,0:T(8,128)} %param.6, f32[8,256,3]{2,1,0:T(8,128)S(1)} %copy.72, f32[8,256,512]{2,1,0:T(8,128)} %param.9, f32[8,256,3]{2,1,0:T(8,128)} %copy.118, f32[8,256,3]{2,1,0:T(8,128)} %copy.120), kind=kLoop, calls=%fused_computation.53 | loop fusion | flops 28366848 | bytes 12664832 | tf_op jit(solution)/shard_map/sub | solution.py:40
  113.4 13.6 %multiply_subtract_fusion.1 = f32[8,256,513]{2,1,0:T(8,128)} fusion(f32[1,262,518]{2,1,0:T(8,128)S(1)} %slice.567, f32[7,262,518]{2,1,0:T(8,128)S(1)} %slice.566, f32[8,262,518]{2,1,0:T(8,128)S(1)} %pad_maximum_fusion, f32[8,256,512]{2,1,0:T(8,128)S(1)} %copy-done.1, f32[8,256,3]{2,1,0:T(8,128)S(1)} %copy-done.21, f32[8,256,3]{2,1,0:T(8,128)S(1)} %copy-done.22), kind=kLoop, calls=%fused_computation.54 | loop fusion | flops 30468096 | bytes 16991360 | tf_op jit(solution)/shard_map/sub | solution.py:40
  134.9 7.5 maximum_maximum_fusion.2
  142.4 22.2 %multiply_subtract_fusion.2 = f32[8,257,512]{2,1,0:T(8,128)} fusion(f32[8,259,518]{2,1,0:T(8,128)} %maximum_maximum_fusion, f32[8,259,518]{2,1,0:T(8,128)} %get-tuple-element.44, f32[8,259,518]{2,1,0:T(8,128)} %get-tuple-element.43), kind=kLoop, calls=%fused_computation.58 | loop fusion | flops 21053440 | bytes 33685504 | tf_op jit(solution)/shard_map/sub | solution.py:40
  172.0 7.9 maximum_maximum_fusion.1
  179.9 26.8 %multiply_subtract_fusion.3 = f32[8,257,512]{2,1,0:T(8,128)} fusion(f32[1,262,518]{2,1,0:T(8,128)} %slice.580, f32[7,262,518]{2,1,0:T(8,128)} %slice.579, f32[8,262,518]{2,1,0:T(8,128)} %copy-done.10, f32[8,259,518]{2,1,0:T(8,128)} %get-tuple-element.50, f32[8,259,518]{2,1,0:T(8,128)} %get-tuple-element.49), kind=kLoop, calls=%fused_computation.59 | loop fusion | flops 24211456 | bytes 38028416 | tf_op jit(solution)/shard_map/sub | solution.py:40
  206.7 23.3 %broadcast_multiply_fusion = (f32[8,256,512]{2,1,0:T(8,128)S(1)}, f32[8,256,512]{2,1,0:T(8,128)}, f32[8,256,512]{2,1,0:T(8,128)}) fusion(f32[8]{0:T(128)S(1)} %copy-done.37, f32[8,256,512]{2,1,0:T(8,128)S(1)} %copy-done.1, f32[8,256,512]{2,1,0:T(8,128)} %param.9, f32[1,256,512]{2,1,0:T(8,128)} %get-tuple-element.58, f32[7,256,512]{2,1,0:T(8,128)S(1)} %slice-done.1, ...), kind=kLoop, calls=%fused_computation.156 | loop fusion | flops 26214400 | bytes 74448992 | tf_op jit(solution)/shard_map/mul | solution.py:168
  232.6 6.6 fusion.16
  244.1 45.0 %all-to-all-done = f32[8,256,512]{2,1,0:T(8,128)} async-done(((f32[8,256,512]{2,1,0:T(8,128)}), f32[8,256,512]{2,1,0:T(8,128)}, u32[]{:S(2)}, u32[]{:S(2)}) %all-to-all-start) | async-done | bytes 4194336 | tf_op jit(solution)/shard_map/all_to_all | solution.py:195
  289.1 7.2 copy.86
  296.3 6.4 reshape.459
  302.7 8.8 fusion.66
  311.6 6.9 add_bitcast_fusion.5
  340.8 98.5 %all_to_all.93 = f32[2,256,2048]{1,0,2:T(2,128)} all-to-all(f32[2,256,2048]{1,0,2:T(2,128)} %reshape.460), channel_id=1, replica_groups=mesh['gx'=4,'gy'=8] {'gy'}, dimensions={2} | all-to-all | bytes 8388608 | tf_op jit(solution)/shard_map/all_to_all | solution.py:196
  439.3 7.2 copy.92
  446.5 9.0 fusion.62
  455.5 7.0 add_bitcast_fusion.3
  477.0 12.2 %copy.98 = f32[2,2048,256]{2,0,1:T(2,128)} copy(f32[2,2048,256]{2,1,0:T(8,128)S(1)} %bitcast.192) | data formatting | bytes 8388608 | tf_op jit(solution)/shard_map/reshape | solution.py:105
  496.0 9.8 %fusion.78 = (f32[1,1,512,256]{3,2,1,0:T(8,128)S(1)}, f32[1,1,512,256]{3,2,1,0:T(8,128)S(1)}, f32[1,1,512,256]{3,2,1,0:T(8,128)S(1)}, f32[1,1,512,256]{3,2,1,0:T...) fusion(f32[]{:T(128)} %bitcast.31, ...), kind=kLoop, calls=%fused_computation.157 | loop fusion | flops 2097152 | bytes 4197436
  513.4 28.3 %all-to-all-done.2 = f32[2,2048,256]{2,0,1:T(2,128)} async-done(((f32[2,2048,256]{2,0,1:T(2,128)}), f32[2,2048,256]{2,0,1:T(2,128)}, u32[]{:S(2)}, u32[]{:S(2)}) %all-to-all-start.2) | async-done | bytes 4194336 | tf_op jit(solution)/shard_map/all_to_all | solution.py:197
  546.8 23.5 %fusion.223 = (f32[131072]{0:T(1024)S(1)}, f32[1,131072]{1,0:T(1,128)S(1)}, f32[1,131072]{1,0:T(1,128)S(1)}, f32[1,131072]{1,0:T(1,128)S(1)}, f32[1,131072]{1,0:...) fusion(f32[1,131072]{1,0:T(1,128)S(1)} %bitcast.209, ...), kind=kLoop, calls=%fused_computation.354 | loop fusion | flops 5898240 | bytes 16777272 | tf_op jit(solution)/shard_map/sub | solution.py:129
  594.4 51.1 %all_to_all.94 = f32[8,512,256]{2,1,0:T(8,128)S(1)} all-to-all(f32[8,512,256]{2,1,0:T(8,128)} %constant_dynamic-update-slice_fusion), channel_id=1, replica_groups=mesh['gx'=4,'gy'=8] {'gx'}, dimensions={0} | all-to-all | bytes 8388608 | tf_op jit(solution)/shard_map/all_to_all | solution.py:206
  651.9 7.2 add_bitcast_fusion.1
  665.0 6.5 multiply_bitcast_fusion.1
  674.0 10.5 %copy.106 = f32[2,2048,256]{2,0,1:T(2,128)S(1)} copy(f32[2,2048,256]{2,1,0:T(8,128)S(1)} %bitcast.195) | data formatting | bytes 8388608 | tf_op jit(solution)/shard_map/div | solution.py:207
  684.4 97.3 %all_to_all.95 = f32[2,2048,256]{2,0,1:T(2,128)} all-to-all(f32[2,2048,256]{2,0,1:T(2,128)S(1)} %copy.106), channel_id=1, replica_groups=mesh['gx'=4,'gy'=8] {'gy'}, dimensions={1} | all-to-all | bytes 8388608 | tf_op jit(solution)/shard_map/all_to_all | solution.py:209
  781.7 9.2 copy.107
  790.9 6.4 reshape.465
  797.3 8.6 fusion.54
  806.0 6.9 add_bitcast_fusion
  835.4 51.5 %all_to_all.96 = f32[2,256,2048]{1,0,2:T(2,128)S(1)} all-to-all(f32[2,256,2048]{1,0,2:T(2,128)} %div.545), channel_id=1, replica_groups=mesh['gx'=4,'gy'=8] {'gx'}, dimensions={2} | all-to-all | bytes 8388608 | tf_op jit(solution)/shard_map/all_to_all | solution.py:211
  909.8 16.2 %divide_subtract_fusion = (f32[8,256,512]{2,1,0:T(8,128)}, f32[8,256,512]{2,1,0:T(8,128)}, f32[8,256,512]{2,1,0:T(8,128)}) fusion(f32[8,256,512]{2,1,0:T(8,128)} %get-tuple-element.28, f32[7,256,512]{2,1,0:T(8,128)} %slice.610, f32[8]{0:T(128)S(1)} %copy-done.39, f32[8,256,512]{2,1,0:T(8,128)} %param.7, f32[8,1,512]{2,1,0:T(1,128)S(1)} %collective-permute-done.13, ...), kind=kLoop, calls=%fused_computation.118 | loop fusion | flops 12582912 | bytes 41418784 | tf_op jit(solution)/shard_map/sub | solution.py:216
  (237 shorter events, 252.5 us)
Async XLA Ops:
  2.9 48.2 %collective-permute-start.1 = (f32[8,256,3]{1,0,2:T(8,128)S(1)}, f32[8,256,3]{1,0,2:T(8,128)S(1)}, u32[]{:S(2)}, u32[]{:S(2)}) collective-permute-start(f32[8,256,3]{1,0,2:T(8,128)S(1)} %copy.128), channel_id=1, source_target_pairs={{0,8},{8,16},{16,24},{24,0},{1,9},{9,17},{17,25},{25,1},{2,10},{10... | collective-permute-start | bytes 73736 | tf_op jit(solution)/shard_map/ppermute | solution.py:25
  6.2 48.2 %collective-permute-start.2 = (f32[8,256,3]{1,0,2:T(8,128)S(1)}, f32[8,256,3]{1,0,2:T(8,128)S(1)}, u32[]{:S(2)}, u32[]{:S(2)}) collective-permute-start(f32[8,256,3]{1,0,2:T(8,128)S(1)} %copy.129), channel_id=1, source_target_pairs={{8,0},{16,8},{24,16},{0,24},{9,1},{17,9},{25,17},{1,25},{10,2},{18... | collective-permute-start | bytes 73736 | tf_op jit(solution)/shard_map/ppermute | solution.py:26
  9.4 84.4 %collective-permute-start.7 = (f32[8,256,3]{1,0,2:T(8,128)S(1)}, f32[8,256,3]{1,0,2:T(8,128)S(1)}, u32[]{:S(2)}, u32[]{:S(2)}) collective-permute-start(f32[8,256,3]{1,0,2:T(8,128)S(1)} %copy.131), channel_id=1, source_target_pairs={{0,8},{8,16},{16,24},{24,0},{1,9},{9,17},{17,25},{25,1},{2,10},{10... | collective-permute-start | bytes 73736 | tf_op jit(solution)/shard_map/ppermute | solution.py:25
  11.4 88.9 %collective-permute-start.8 = (f32[8,256,3]{1,0,2:T(8,128)}, f32[8,256,3]{1,0,2:T(8,128)}, u32[]{:S(2)}, u32[]{:S(2)}) collective-permute-start(f32[8,256,3]{1,0,2:T(8,128)} %copy.132), channel_id=1, source_target_pairs={{8,0},{16,8},{24,16},{0,24},{9,1},{17,9},{25,17},{1,25},{10,2},{18... | collective-permute-start | bytes 73736 | tf_op jit(solution)/shard_map/ppermute | solution.py:26
  16.5 40.1 %collective-permute-start = (f32[8,256,3]{1,0,2:T(8,128)S(1)}, f32[8,256,3]{1,0,2:T(8,128)S(1)}, u32[]{:S(2)}, u32[]{:S(2)}) collective-permute-start(f32[8,256,3]{1,0,2:T(8,128)S(1)} %copy.127), channel_id=1, source_target_pairs={{0,8},{8,16},{16,24},{24,0},{1,9},{9,17},{17,25},{25,1},{2,10},{10... | collective-permute-start | bytes 73736 | tf_op jit(solution)/shard_map/ppermute | solution.py:25
  27.1 13.7 %copy-start.36 = (f32[8]{0:T(128)}, f32[8]{0:T(128)S(1)}, u32[]{:S(2)}) copy-start(f32[8]{0:T(128)S(1)} %get-tuple-element.31) | copy-start | bytes 100
  27.1 13.7 %copy-start.38 = (f32[8]{0:T(128)}, f32[8]{0:T(128)S(1)}, u32[]{:S(2)}) copy-start(f32[8]{0:T(128)S(1)} %get-tuple-element.30) | copy-start | bytes 100
  51.1 7.4 collective-permute-start.14
  54.4 5.6 collective-permute-start.15
  56.6 33.3 %collective-permute-start.4 = (f32[8,256,3]{1,0,2:T(8,128)S(1)}, f32[8,256,3]{1,0,2:T(8,128)}, u32[]{:S(2)}, u32[]{:S(2)}) collective-permute-start(f32[8,256,3]{1,0,2:T(8,128)S(1)} %copy.130), channel_id=1, source_target_pairs={{8,0},{16,8},{24,16},{0,24},{9,1},{17,9},{25,17},{1,25},{10,2},{18... | collective-permute-start | bytes 73736 | tf_op jit(solution)/shard_map/ppermute | solution.py:26
  58.4 49.5 %copy-start.15 = (f32[8,256,3]{2,1,0:T(8,128)}, f32[8,256,3]{2,1,0:T(8,128)S(1)}, u32[]{:S(2)}) copy-start(f32[8,256,3]{2,1,0:T(8,128)S(1)} %copy.72) | copy-start | bytes 73732
  58.5 68.5 %collective-permute-start.3 = (f32[8,3,518]{2,1,0:T(4,128)}, f32[8,3,518]{2,1,0:T(4,128)S(1)}, u32[]{:S(2)}, u32[]{:S(2)}) collective-permute-start(f32[8,3,518]{2,1,0:T(4,128)} %get-tuple-element.54), channel_id=1, source_target_pairs={{0,1},{1,2},{2,3},{3,4},{4,5},{5,6},{6,7},{7,0},{8,9},{9,10},{10,1... | collective-permute-start | bytes 149192 | tf_op jit(solution)/shard_map/ppermute | solution.py:25
  60.5 104.1 %collective-permute-start.9 = (f32[8,3,518]{2,1,0:T(4,128)S(1)}, f32[8,3,518]{2,1,0:T(4,128)S(1)}, u32[]{:S(2)}, u32[]{:S(2)}) collective-permute-start(f32[8,3,518]{2,1,0:T(4,128)S(1)} %get-tuple-element.53), channel_id=1, source_target_pairs={{1,0},{2,1},{3,2},{4,3},{5,4},{6,5},{7,6},{0,7},{9,8},{10,9},{11,1... | collective-permute-start | bytes 149192 | tf_op jit(solution)/shard_map/ppermute | solution.py:26
  66.1 22.9 %copy-start.3 = (f32[8,256,512]{2,1,0:T(8,128)S(1)}, f32[8,256,512]{2,1,0:T(8,128)}, u32[]{:S(2)}) copy-start(f32[8,256,512]{2,1,0:T(8,128)} %param.9) | copy-start | bytes 12582916
  66.1 22.9 %copy-start.17 = (f32[8,256,3]{2,1,0:T(8,128)S(1)}, f32[8,256,3]{2,1,0:T(8,128)}, u32[]{:S(2)}) copy-start(f32[8,256,3]{2,1,0:T(8,128)} %copy.118) | copy-start | bytes 73732
  66.1 22.9 %copy-start.19 = (f32[8,256,3]{2,1,0:T(8,128)S(1)}, f32[8,256,3]{2,1,0:T(8,128)}, u32[]{:S(2)}) copy-start(f32[8,256,3]{2,1,0:T(8,128)} %copy.120) | copy-start | bytes 73732
  93.8 10.6 %collective-permute-start.5 = (f32[8,3,518]{2,1,0:T(4,128)}, f32[8,3,518]{2,1,0:T(4,128)S(1)}, u32[]{:S(2)}, u32[]{:S(2)}) collective-permute-start(f32[8,3,518]{2,1,0:T(4,128)} %get-tuple-element.47), channel_id=1, source_target_pairs={{0,1},{1,2},{2,3},{3,4},{4,5},{5,6},{6,7},{7,0},{8,9},{9,10},{10,1... | collective-permute-start | bytes 149192 | tf_op jit(solution)/shard_map/ppermute | solution.py:25
  94.4 13.5 %collective-permute-start.6 = (f32[8,3,518]{2,1,0:T(4,128)}, f32[8,3,518]{2,1,0:T(4,128)S(1)}, u32[]{:S(2)}, u32[]{:S(2)}) collective-permute-start(f32[8,3,518]{2,1,0:T(4,128)} %get-tuple-element.48), channel_id=1, source_target_pairs={{1,0},{2,1},{3,2},{4,3},{5,4},{6,5},{7,6},{0,7},{9,8},{10,9},{11,1... | collective-permute-start | bytes 149192 | tf_op jit(solution)/shard_map/ppermute | solution.py:26
  104.4 67.6 %collective-permute-start.10 = (f32[8,3,518]{2,1,0:T(4,128)}, f32[8,3,518]{2,1,0:T(4,128)}, u32[]{:S(2)}, u32[]{:S(2)}) collective-permute-start(f32[8,3,518]{2,1,0:T(4,128)} %get-tuple-element.51), channel_id=1, source_target_pairs={{0,1},{1,2},{2,3},{3,4},{4,5},{5,6},{6,7},{7,0},{8,9},{9,10},{10,1... | collective-permute-start | bytes 149192 | tf_op jit(solution)/shard_map/ppermute | solution.py:25
  104.4 67.6 %collective-permute-start.11 = (f32[8,3,518]{2,1,0:T(4,128)}, f32[8,3,518]{2,1,0:T(4,128)}, u32[]{:S(2)}, u32[]{:S(2)}) collective-permute-start(f32[8,3,518]{2,1,0:T(4,128)} %get-tuple-element.52), channel_id=1, source_target_pairs={{1,0},{2,1},{3,2},{4,3},{5,4},{6,5},{7,6},{0,7},{9,8},{10,9},{11,1... | collective-permute-start | bytes 149192 | tf_op jit(solution)/shard_map/ppermute | solution.py:26
  107.9 27.0 %collective-permute-start.16 = (f32[8,3,518]{2,1,0:T(4,128)S(1)}, f32[8,3,518]{2,1,0:T(4,128)S(1)}, u32[]{:S(2)}, u32[]{:S(2)}) collective-permute-start(f32[8,3,518]{2,1,0:T(4,128)S(1)} %copy-done.32), channel_id=1, source_target_pairs={{0,1},{1,2},{2,3},{3,4},{4,5},{5,6},{6,7},{7,0},{8,9},{9,10},{10,1... | collective-permute-start | bytes 149192 | tf_op jit(solution)/shard_map/ppermute | solution.py:25
  113.4 17.2 %copy-start.5 = (f32[8,256,512]{2,1,0:T(8,128)S(1)}, f32[8,256,512]{2,1,0:T(8,128)}, u32[]{:S(2)}) copy-start(f32[8,256,512]{2,1,0:T(8,128)} %param.7) | copy-start | bytes 12582916
  127.0 7.9 collective-permute-start.17
  179.9 26.8 %slice-start.1 = ((f32[8,256,512]{2,1,0:T(8,128)}), f32[7,256,512]{2,1,0:T(8,128)S(1)}, s32[]{:S(2)}) async-start(f32[8,256,512]{2,1,0:T(8,128)} %param.9), calls=%async_computation.7 | async-start | bytes 7340032 | tf_op jit(solution)/shard_map/slice | solution.py:32
  179.9 26.8 %copy-start.37 = (f32[8]{0:T(128)S(1)}, f32[8]{0:T(128)}, u32[]{:S(2)}) copy-start(f32[8]{0:T(128)} %copy-done.36) | copy-start | bytes 100
  179.9 26.8 %copy-start.44 = (f32[8]{0:T(128)S(1)}, f32[8]{0:T(128)}, u32[]{:S(2)}) copy-start(f32[8]{0:T(128)} %get-tuple-element.34) | copy-start | bytes 100
  179.9 26.8 %copy-start.45 = (f32[8]{0:T(128)S(1)}, f32[8]{0:T(128)}, u32[]{:S(2)}) copy-start(f32[8]{0:T(128)} %get-tuple-element.29) | copy-start | bytes 100
  206.7 23.9 %copy-start.8 = (f32[8,256,512]{2,1,0:T(8,128)S(1)}, f32[8,256,512]{2,1,0:T(8,128)}, u32[]{:S(2)}) copy-start(f32[8,256,512]{2,1,0:T(8,128)} %param.6) | copy-start | bytes 12582916
  239.2 49.9 %all-to-all-start = ((f32[8,256,512]{2,1,0:T(8,128)}), f32[8,256,512]{2,1,0:T(8,128)}, u32[]{:S(2)}, u32[]{:S(2)}) async-start(f32[8,256,512]{2,1,0:T(8,128)} %fusion.16), calls=%async_computation | async-start | bytes 8388608 | tf_op jit(solution)/shard_map/all_to_all | solution.py:195
  489.2 52.5 %all-to-all-start.2 = ((f32[2,2048,256]{2,0,1:T(2,128)}), f32[2,2048,256]{2,0,1:T(2,128)}, u32[]{:S(2)}, u32[]{:S(2)}) async-start(f32[2,2048,256]{2,0,1:T(2,128)} %copy.98), calls=%async_computation.2 | async-start | bytes 8388608 | tf_op jit(solution)/shard_map/all_to_all | solution.py:197
  895.4 14.5 %collective-permute-start.13 = (f32[8,1,512]{2,1,0:T(1,128)S(1)}, f32[8,1,512]{2,1,0:T(1,128)S(1)}, u32[]{:S(2)}, u32[]{:S(2)}) collective-permute-start(f32[8,1,512]{2,1,0:T(1,128)S(1)} %slice.609), channel_id=1, source_target_pairs={{0,7},{1,0},{2,1},{3,2},{4,3},{5,4},{6,5},{7,6},{8,15},{9,8},{10,9... | collective-permute-start | bytes 49160 | tf_op jit(solution)/shard_map/ppermute | solution.py:15
  897.4 12.1 %collective-permute-start.12 = (f32[8,256,1]{1,0,2:T(8,128)S(1)}, f32[8,256,1]{1,0,2:T(8,128)S(1)}, u32[]{:S(2)}, u32[]{:S(2)}) collective-permute-start(f32[8,256,1]{1,0,2:T(8,128)S(1)} %copy.115), channel_id=1, source_target_pairs={{0,24},{8,0},{16,8},{24,16},{1,25},{9,1},{17,9},{25,17},{2,26},{10... | collective-permute-start | bytes 24584 | tf_op jit(solution)/shard_map/ppermute | solution.py:15
  (36 other events, 178.4 us)
where the time goes:
time: 937 us; the launch traced here: 926 us
  blocking collectives  298 us (32%)
  other arithmetic  219 us (23%)
  local copies, waits for them, and re-layouts  186 us (20%)
  matrix products  109 us (12%)
  waiting for transfers between devices  73.4 us (8%)
  starting transfers between devices  38.3 us (4%)
    all_to_all x1, blocking collectives, per_device(): lax.all_to_all(lines, 'gy', split_axis=2, concat_axis=1, tiled=True)  98.5 us
    all_to_all x1, blocking collectives, per_device(): lax.all_to_all(back_y, 'gy', split_axis=1, concat_axis=2, tiled=True)  97.3 us
    sub x4, other arithmetic, upwind_flux(): return centred - damped  85.5 us
    all_to_all x1, blocking collectives, per_device(): lax.all_to_all(rows_x, 'gx', split_axis=2, concat_axis=0, tiled=True)  51.5 us
    all_to_all x1, blocking collectives, per_device(): lax.all_to_all(solution, 'gx', split_axis=0, concat_axis=1, tiled=True)  51.1 us
    all_to_all x1, waiting for transfers between devices, per_device(): lax.all_to_all(source_term, 'gx', split_axis=0, concat_axis=2, tiled=True)  45 us
    sub x4, other arithmetic, tridiag_solve(): partial_sols[level] - ratios[level] * solved_levels[-1]  32.8 us
    dot_general x4, matrix products, hartley_axis(): imag_part = -jnp.einsum(first_form, shaped, sin_q, precision=high)  32.5 us
  transfers between devices with their start and end apart: 20, of which 2 were waited for; matrix products, arithmetic and copies ran while one was open for 18% of the time, Pallas kernels for 0%

commit v1 on v0

v1 whole, which is shorter than its diff:
```python
import math

import jax
import jax.numpy as jnp
import numpy as np
from jax import lax
from jax.experimental import pallas as pl
from jax.experimental.pallas import tpu as pltpu
from jax.sharding import PartitionSpec as P

time_step = 0.2
buoyancy_gain = 1.0


def from_behind(value, axis, steps):
    count = lax.axis_size(axis)
    pairs = [(source, (source + steps) % count) for source in range(count)]
    return lax.ppermute(value, axis, pairs)


def extended(value, sides, width):
    for axis, dim in sides:
        size, length = (lax.axis_size(axis), value.shape[dim])
        up = [(i, (i + 1) % size) for i in range(size)]
        down = [(j, i) for i, j in up]
        last = lax.slice_in_dim(value, length - width, length, axis=dim)
        first = lax.slice_in_dim(value, 0, width, axis=dim)
        before = lax.ppermute(last, axis, up)
        after = lax.ppermute(first, axis, down)
        value = jnp.concatenate([before, value, after], axis=dim)
    return value


def lift_level(field):
    return jnp.concatenate([field[1:], field[-1:]], axis=0)


def upwind_flux(q_m2, q_m1, q_zero, q_p1, q_p2, q_p3, velocity):
    centred = velocity * (37.0 * (q_zero + q_p1) - 8.0 * (q_m1 + q_p2) + (q_m2 + q_p3)) / 60.0
    damped = (
        jnp.abs(velocity) * (10.0 * (q_p1 - q_zero) - 5.0 * (q_p2 - q_m1) + (q_p3 - q_m2)) / 60.0
    )
    return centred - damped


def vertical_tend(tracer, velocity, rho_face, rho_level, spacing):
    levels = tracer.shape[0]
    padded = jnp.pad(tracer, ((2, 3), (0, 0), (0, 0)), mode="edge")
    parts = [padded[2 + offset : 2 + offset + levels] for offset in range(-2, 4)]
    flux_z = upwind_flux(*parts, velocity) * rho_face[:, None, None]
    below = jnp.concatenate([jnp.zeros_like(flux_z[:1]), flux_z[:-1]], axis=0)
    return -(flux_z - below) / (rho_level * spacing)[:, None, None]


def horizontal_local(tracer_rim, u_rim, v_rim, rows_y, cols_x):
    row_band = tracer_rim[:, 3 : 3 + rows_y, :]
    parts_x = [row_band[:, :, 2 + offset : 3 + offset + cols_x] for offset in range(-2, 4)]
    flux_x = upwind_flux(*parts_x, u_rim[:, 3 : 3 + rows_y, 2 : 3 + cols_x])
    col_band = tracer_rim[:, :, 3 : 3 + cols_x]
    parts_y = [col_band[:, 2 + offset : 3 + offset + rows_y, :] for offset in range(-2, 4)]
    flux_y = upwind_flux(*parts_y, v_rim[:, 2 : 3 + rows_y, 3 : 3 + cols_x])
    return -(flux_x[:, :, 1:] - flux_x[:, :, :-1]) - (flux_y[:, 1:, :] - flux_y[:, :-1, :])


high = lax.Precision.HIGHEST
vmem_bytes = 48 * 1024 * 1024
jacobi_sweeps = 8


def power(base, exponent):
    result = None
    while exponent:
        if exponent & 1:
            result = base if result is None else result * base
        exponent >>= 1
        if exponent:
            base = base * base
    return result


def jacobi_kernel(columns_ref, basis_ref, square_ref):
    levels = columns_ref.shape[0]
    rows = lax.broadcasted_iota(jnp.int32, columns_ref.shape[1:], 0)

    def sweep(_, state):
        factor, basis = list(state[0]), list(state[1])
        order = list(range(levels))
        for _round in range(levels - 1):
            for slot in range(levels // 2):
                i, j = sorted((order[slot], order[levels - 1 - slot]))
                norm_i = jnp.sum(factor[i] * factor[i], axis=0, keepdims=True)
                norm_j = jnp.sum(factor[j] * factor[j], axis=0, keepdims=True)
                cross = jnp.sum(factor[i] * factor[j], axis=0, keepdims=True)
                gap = norm_j - norm_i
                size = jnp.abs(gap) + jnp.sqrt(gap * gap + 4.0 * cross * cross)
                twice = jnp.where(gap < 0.0, -2.0 * cross, 2.0 * cross)
                tangent = jnp.where(size > 0.0, twice / jnp.where(size > 0.0, size, 1.0), 0.0)
                cosine = 1.0 / jnp.sqrt(1.0 + tangent * tangent)
                sine = cosine * tangent
                for held in (factor, basis):
                    left, right = held[i], held[j]
                    held[i] = cosine * left - sine * right
                    held[j] = sine * left + cosine * right
            order = [order[0], order[-1]] + order[1:-1]
        return tuple(factor), tuple(basis)

    start = (
        tuple(columns_ref[i] for i in range(levels)),
        tuple(jnp.where(rows == i, 1.0, 0.0) for i in range(levels)),
    )
    factor, basis = lax.fori_loop(0, jacobi_sweeps, sweep, start)
    for i in range(levels):
        basis_ref[i] = basis[i]
        square_ref[i] = jnp.broadcast_to(
            jnp.sum(factor[i] * factor[i], axis=0, keepdims=True), columns_ref.shape[1:]
        )


def vertical_modes(density, thickness, face_density, face_spacing):
    levels = density.shape[0]
    mass = density * thickness
    stiff = face_density / face_spacing
    diagonal = -jnp.sqrt(stiff / mass)
    beside = jnp.sqrt(stiff / jnp.concatenate([mass[1:], mass[-1:]]))
    factor = diagonal[:, None] * np.eye(levels, dtype=np.float32)
    factor = factor + beside[:, None] * np.eye(levels, k=1, dtype=np.float32)
    shape = jax.ShapeDtypeStruct((levels, levels, 128), jnp.float32)
    basis, square = pl.pallas_call(
        jacobi_kernel, out_shape=(shape, shape), name="vertical_modes"
    )(jnp.broadcast_to(factor.T[:, :, None], shape.shape))
    root_mass = jnp.sqrt(mass)[None, :]
    return basis[:, :, 0] * root_mass, basis[:, :, 0] / root_mass, square[:, 0, 0]


def decay_of(excess):
    return 1.0 / (1.0 + 0.5 * excess + jnp.sqrt(excess + 0.25 * excess * excess))


def sine_matrix(count):
    index = np.arange(count)
    matrix = np.sqrt(2.0 / count) * np.sin(np.pi * np.outer(index, index) % (2 * np.pi * count) / count)
    matrix[0, 0] = 1.0
    return matrix.astype(np.float32)


def edge_weights(count):
    matrix = sine_matrix(count)
    weights = np.zeros((count, 128), np.float32)
    weights[1:, 0] = matrix[1, 1:]
    weights[1:, 1] = matrix[count - 1, 1:]
    return weights


def run_sweeps(source, decay_ref, start_ref, work_ref, ends_ref, rows, levels):
    decay = decay_ref[...]

    def forward(j, carry):
        at = pl.ds(pl.multiple_of(j * levels, levels), levels)
        value = carry + source(at)
        scaled = decay * value
        work_ref[at, :] = scaled
        return scaled

    last = lax.fori_loop(0, rows, forward, jnp.zeros_like(decay), unroll=4)
    top = start_ref[...] * last
    ends_ref[0] = top
    work_ref[pl.ds((rows - 1) * levels, levels), :] = top

    def backward(step, carry):
        at = pl.ds(pl.multiple_of((rows - 2 - step) * levels, levels), levels)
        value = decay * carry - work_ref[at, :]
        work_ref[at, :] = value
        return value

    ends_ref[1] = lax.fori_loop(0, rows - 1, backward, top, unroll=4)


def first_kernel(modes_ref, sine_ref, weight_ref, decay_ref, start_ref, spectral_ref, edge_ref, ends_ref, work_ref):
    total, count = modes_ref.shape
    levels = decay_ref.shape[0]
    chunk = min(256, total)

    @pl.loop(0, total // chunk)
    def _(step):
        at = pl.ds(pl.multiple_of(step * chunk, chunk), chunk)
        spectral_ref[at, :] = jnp.dot(modes_ref[at, :], sine_ref[...], precision=high)

    run_sweeps(lambda at: spectral_ref[at, :], decay_ref, start_ref, work_ref, ends_ref, total // levels, levels)

    @pl.loop(0, total // chunk)
    def _(step):
        at = pl.ds(pl.multiple_of(step * chunk, chunk), chunk)
        lane = lax.broadcasted_iota(jnp.int32, (chunk, 128), 1)
        near = jnp.where(lane == 0, spectral_ref[at, 0:128], 0.0)
        edge_ref[at, :] = near - jnp.dot(work_ref[at, :], weight_ref[...], precision=high)


def coupled_terms(decay_ref, ends_ref, work_ref, rows, levels):
    decay = decay_ref[...]

    def upward(j, carry):
        at = pl.ds(pl.multiple_of(j * levels, levels), levels)
        value = decay * carry
        work_ref[at, :] += value
        return value

    lax.fori_loop(0, rows, upward, ends_ref[0], unroll=4)

    def downward(step, carry):
        at = pl.ds(pl.multiple_of((rows - 1 - step) * levels, levels), levels)
        value = decay * carry
        work_ref[at, :] += value
        return value

    lax.fori_loop(0, rows, downward, ends_ref[1], unroll=4)


def second_kernel(decay_ref, ends_ref, weight_ref, edge_in_ref, edge_ref, work_ref):
    total, _ = work_ref.shape
    levels = decay_ref.shape[0]
    chunk = min(256, total)
    work_ref[...] = jnp.zeros_like(work_ref)
    coupled_terms(decay_ref, ends_ref, work_ref, total // levels, levels)

    @pl.loop(0, total // chunk)
    def _(step):
        at = pl.ds(pl.multiple_of(step * chunk, chunk), chunk)
        edge_ref[at, :] = edge_in_ref[at, :] - jnp.dot(work_ref[at, :], weight_ref[...], precision=high)


def third_kernel(spectral_ref, line_ref, spread_ref, decay_ref, start_ref, free_ref, ends_ref, work_ref):
    total, _ = spectral_ref.shape
    levels = decay_ref.shape[0]
    chunk = min(256, total)

    @pl.loop(0, total // chunk)
    def _(step):
        at = pl.ds(pl.multiple_of(step * chunk, chunk), chunk)
        work_ref[at, :] = spectral_ref[at, :] - jnp.dot(line_ref[at, :], spread_ref[...], precision=high)

    run_sweeps(lambda at: work_ref[at, :], decay_ref, start_ref, free_ref, ends_ref, total // levels, levels)


def fourth_kernel(free_ref, line_ref, sine_ref, decay_ref, ends_ref, out_ref, work_ref):
    total, count = free_ref.shape
    levels = decay_ref.shape[0]
    chunk = min(256, total)
    work_ref[...] = free_ref[...]
    coupled_terms(decay_ref, ends_ref, work_ref, total // levels, levels)

    @pl.loop(0, total // chunk)
    def _(step):
        at = pl.ds(pl.multiple_of(step * chunk, chunk), chunk)
        lane = lax.broadcasted_iota(jnp.int32, (chunk, count), 1)
        column = jnp.broadcast_to(line_ref[at, 0:1], (chunk, count))
        full = jnp.where(lane == 0, column, work_ref[at, :])
        out_ref[at, :] = jnp.dot(full, sine_ref[...], precision=high)


def couple(ends, ratio):
    groups, here = lax.axis_size("gy"), lax.axis_index("gy")
    gathered = lax.all_gather(ends, "gy")
    block = jnp.arange(groups, dtype=jnp.int32)
    scale = 1.0 / (1.0 - power(ratio, groups))

    def weighted(values, exponent):
        factor, base, bit = jnp.ones_like(values), ratio, 1
        while bit < groups:
            factor = jnp.where((exponent & bit)[:, None, None] > 0, factor * base, factor)
            base, bit = base * base, bit * 2
        return jnp.sum(values * factor, axis=0) * scale

    from_low = weighted(gathered[:, 0], (here - 1 - block + 2 * groups) % groups)
    from_high = weighted(gathered[:, 1], (block - here - 1 + 2 * groups) % groups)
    return jnp.stack([from_low, from_high])


def split_count(count):
    inner = 2 ** ((count.bit_length() - 1) // 2)
    return count // inner, inner


def twiddles(rows, cols, count):
    angles = 2.0 * np.pi * (np.outer(np.arange(rows), np.arange(cols)) % count) / count
    return np.cos(angles).astype(np.float32), np.sin(angles).astype(np.float32)


def hartley_lines(lines):
    count = lines.shape[-1]
    outer, inner = split_count(count)
    shaped = lines.reshape(lines.shape[:-1] + (outer, inner))
    cos_q, sin_q = twiddles(outer, outer, outer)
    cos_t, sin_t = twiddles(outer, inner, count)
    cos_p, sin_p = twiddles(inner, inner, inner)
    real = jnp.einsum("aqp,mq->amp", shaped, cos_q, precision=high)
    imag = -jnp.einsum("aqp,mq->amp", shaped, sin_q, precision=high)
    turned_re = real * cos_t + imag * sin_t
    turned_im = imag * cos_t - real * sin_t
    result = jnp.einsum("amp,pn->amn", turned_re, cos_p + sin_p, precision=high)
    return result + jnp.einsum("amp,pn->amn", turned_im, sin_p - cos_p, precision=high)


def hartley_back(spectra):
    outer, inner = spectra.shape[-2:]
    count = outer * inner
    cos_q, sin_q = twiddles(outer, outer, outer)
    cos_t, sin_t = twiddles(outer, inner, count)
    cos_p, sin_p = twiddles(inner, inner, inner)
    real = jnp.einsum("amn,np->amp", spectra, cos_p, precision=high)
    imag = -jnp.einsum("amn,np->amp", spectra, sin_p, precision=high)
    turned_re = real * cos_t + imag * sin_t
    turned_im = imag * cos_t - real * sin_t
    result = jnp.einsum("amp,qm->aqp", turned_re, cos_q + sin_q, precision=high)
    result = result + jnp.einsum("amp,qm->aqp", turned_im, sin_q - cos_q, precision=high)
    return result.reshape(spectra.shape[:-2] + (count,)) / count


def separator_solve(edge, square, rows, cols_x):
    groups_x, groups_y = lax.axis_size("gx"), lax.axis_size("gy")
    levels = square.shape[0]
    count = groups_y * rows
    sides = edge.reshape(rows, levels, 128)[:, :, :2].transpose(2, 1, 0)
    lines = lax.all_gather(sides, ("gx", "gy"))
    lines = lines.reshape(groups_x, groups_y, 2, levels, rows).transpose(2, 0, 3, 1, 4)
    residual = (lines[0] + jnp.roll(lines[1], 1, axis=0)).reshape(groups_x * levels, count)
    spectra = hartley_lines(residual)
    outer, inner = split_count(count)
    index = np.arange(outer)[:, None] + outer * np.arange(inner)[None, :]
    excess = (4.0 * np.sin(np.pi * index / count) ** 2).astype(np.float32) + square[:, None, None]
    ratio = power(decay_of(excess), cols_x)
    scale = -1.0 / ((1.0 - power(ratio, groups_x)) * jnp.sqrt(excess * (excess + 4.0)))
    powers = [jnp.ones_like(ratio)]
    for _ in range(groups_x):
        powers.append(powers[-1] * ratio)
    here = lax.axis_index("gx")
    spectra = spectra.reshape(groups_x, levels, outer, inner)
    twice = jnp.concatenate([spectra, spectra, spectra[:1]], axis=0)
    ahead = lax.dynamic_slice_in_dim(twice, here, groups_x + 1, axis=0)
    own = sum((powers[d] + powers[groups_x - d]) * ahead[d] for d in range(groups_x))
    east = sum((powers[d] + powers[groups_x - d]) * ahead[d + 1] for d in range(groups_x))
    solved = jnp.stack([own * scale, east * scale]).reshape(2 * levels, outer, inner)
    whole = hartley_back(solved).reshape(2, levels, count)
    mine = lax.dynamic_slice_in_dim(whole, lax.axis_index("gy") * rows, rows, axis=2)
    flat = mine.transpose(2, 1, 0).reshape(rows * levels, 2)
    return jnp.pad(flat, ((0, 0), (0, 126)))


def pressure_modes(modes, square):
    total, cols_x = modes.shape
    levels = square.shape[0]
    rows = total // levels
    sine = sine_matrix(cols_x)
    weight = edge_weights(cols_x)
    index = np.arange(cols_x)
    excess = (4.0 * np.sin(np.pi * index / (2 * cols_x)) ** 2).astype(np.float32) + square[:, None]
    decay = jnp.where(index[None, :] > 0, decay_of(excess), 0.0)
    start = -1.0 / (1.0 - decay * decay)
    ratio = power(decay, rows)
    big = jax.ShapeDtypeStruct((total, cols_x), jnp.float32)
    strip = jax.ShapeDtypeStruct((total, 128), jnp.float32)
    ends = jax.ShapeDtypeStruct((2, levels, cols_x), jnp.float32)
    scratch = [pltpu.VMEM((total, cols_x), jnp.float32)]
    params = pltpu.CompilerParams(vmem_limit_bytes=vmem_bytes)

    def call(kernel, outs, name):
        return pl.pallas_call(kernel, out_shape=outs, scratch_shapes=scratch, compiler_params=params, name=name)

    spectral, edge, free_ends = call(first_kernel, (big, strip, ends), "first_solve")(
        modes, sine, weight, decay, start
    )
    edge = call(second_kernel, strip, "edge_terms")(decay, couple(free_ends, ratio), weight, edge)
    lines = separator_solve(edge, square, rows, cols_x)
    free, free_ends = call(third_kernel, (big, ends), "second_solve")(
        spectral, lines, weight.T, decay, start
    )
    return call(fourth_kernel, big, "to_columns")(free, lines, sine, decay, couple(free_ends, ratio))


def shift_gradient(pressure):
    east_cells = from_behind(pressure[:, :, :1], "gx", -1)
    north_cells = from_behind(pressure[:, :1, :], "gy", -1)
    grad_x = jnp.concatenate([pressure[:, :, 1:], east_cells], axis=2) - pressure
    grad_y = jnp.concatenate([pressure[:, 1:, :], north_cells], axis=1) - pressure
    return (grad_x, grad_y)


def per_device(u_face, v_face, w_face, theta_field, density, thickness):
    levels, rows_y, cols_x = theta_field.shape
    theta_rim, w_rim, u_rim, v_rim = (
        extended(theta_field, (("gx", 2), ("gy", 1)), 3),
        extended(w_face, (("gx", 2), ("gy", 1)), 3),
        extended(u_face, (("gx", 2), ("gy", 1)), 3),
        extended(v_face, (("gx", 2), ("gy", 1)), 3),
    )
    face_density = (density + lift_level(density)) / 2.0
    face_spacing = (thickness + lift_level(thickness)) / 2.0
    forward, back, square = vertical_modes(density, thickness, face_density, face_spacing)
    adv_theta = horizontal_local(theta_rim, u_rim, v_rim, rows_y, cols_x) + vertical_tend(
        theta_field, w_face, face_density, density, thickness
    )
    u_level = (u_rim + lift_level(u_rim)) / 2.0
    v_level = (v_rim + lift_level(v_rim)) / 2.0
    w_level = (w_face + lift_level(w_face)) / 2.0
    adv_w = horizontal_local(w_rim, u_level, v_level, rows_y, cols_x) + vertical_tend(
        w_face, w_level, lift_level(density), face_density, face_spacing
    )
    theta_new = theta_field + time_step * adv_theta
    w_star = w_face + time_step * (
        adv_w + buoyancy_gain * (theta_field + lift_level(theta_field)) / 2.0
    )
    mass_flux = face_density[:, None, None] * w_star
    mass_below = jnp.concatenate([jnp.zeros_like(mass_flux[:1]), mass_flux[:-1]], axis=0)
    divergence = (
        u_face
        - u_rim[:, 3 : 3 + rows_y, 2 : 2 + cols_x]
        + (v_face - v_rim[:, 2 : 2 + rows_y, 3 : 3 + cols_x])
    )
    divergence = divergence + (mass_flux - mass_below) / (density * thickness)[:, None, None]
    source_term = divergence / time_step
    modes = jnp.einsum("kl,lyx->ykx", forward, source_term, precision=high)
    solved = pressure_modes(modes.reshape(rows_y * levels, cols_x), square)
    pressure = jnp.einsum("kl,ykx->lyx", back, solved.reshape(rows_y, levels, cols_x), precision=high)
    grad_x, grad_y = shift_gradient(pressure)
    u_new = u_face - time_step * grad_x
    v_new = v_face - time_step * grad_y
    above = jnp.concatenate([pressure[1:], jnp.zeros_like(pressure[:1])], axis=0)
    w_new = w_star - time_step * (above - pressure) / face_spacing[:, None, None]
    return (u_new, v_new, w_new, theta_new, pressure)


def solution(mesh):
    blocks = P(None, "gy", "gx")
    return jax.shard_map(
        per_device,
        mesh=mesh,
        in_specs=(blocks, blocks, blocks, blocks, P(), P()),
        out_specs=(blocks,) * 5,
        check_vma=False,
    )
```

time: 937 us -> 457 us (0.49)
  blocking collectives: 298 us -> 68.6 us
  local copies, waits for them, and re-layouts: 186 us -> 96.5 us
  matrix products: 109 us -> 26.5 us
  waiting for transfers between devices: 73.4 us -> 0.05 us
  Pallas kernels: 0 us -> 53.8 us
  other arithmetic: 219 us -> 179 us
  starting transfers between devices: 38.3 us -> 27 us
    all_to_all x4 -> x0, blocking collectives: 298 us -> none  [the longest x1 98.5 us: per_device(): lax.all_to_all(lines, 'gy', split_axis=2, concat_axis=1, tiled=True)]
    dot_general x16 -> x10, matrix products: 109 us -> 26.5 us  [the longest x1 13.6 us: per_device(): modes = jnp.einsum('kl,lyx->ykx', forward, source_term, precision=high)]
    all_to_all x2 -> x0, waiting for transfers between devices: 73.3 us -> none  [the longest x1 45 us: per_device(): lax.all_to_all(source_term, 'gx', split_axis=0, concat_axis=2, tiled=True)]
    all_gather x0 -> x3, blocking collectives: none -> 68.6 us  [the longest x1 40 us: separator_solve(): lines = lax.all_gather(sides, ('gx', 'gy'))]
    pallas_call x0 -> x5, Pallas kernels: none -> 53.8 us  [the longest x1 18.7 us: pressure_modes(): call(first_kernel, (big, strip, ends), 'first_solve')]
    all_to_all x7 -> x0, local copies, waits for them, and re-layouts: 34 us -> none  [the longest x1 9.18 us: per_device(): lax.all_to_all(back_y, 'gy', split_axis=1, concat_axis=2, tiled=True)]
    sub x4 -> x0, other arithmetic: 32.8 us -> none  [tridiag_solve(): partial_sols[level] - ratios[level] * solved_levels[-1]]
    reshape x4 -> x0, local copies, waits for them, and re-layouts: 30.9 us -> none  [the longest x2 18.1 us: hartley_axis(): return result.reshape(shape)]
  transfers between devices with their start and end apart: 20 -> 18, of which waited for: 2 -> 0; matrix products, arithmetic and copies ran while one was open for 18% -> 39% of each run, Pallas kernels for 0% -> 1%
where the time goes in v1:
time: 457 us; the launch traced here: 454 us
  other arithmetic  179 us (39%)
  local copies, waits for them, and re-layouts  96.5 us (21%)
  blocking collectives  68.6 us (15%)
  Pallas kernels  53.8 us (12%)
  starting transfers between devices  27 us (6%)
  matrix products  26.5 us (6%)
    sub x4, other arithmetic, upwind_flux(): return centred - damped  75.9 us
    unnamed x173, local copies, waits for them, and re-layouts  48.2 us
    all_gather x1, blocking collectives, separator_solve(): lines = lax.all_gather(sides, ('gx', 'gy'))  40 us
    mul x1, other arithmetic, per_device(): mass_flux = face_density[:, None, None] * w_star  30.3 us
    all_gather x2, blocking collectives, couple(): gathered = lax.all_gather(ends, 'gy')  28.7 us
    concatenate x6, other arithmetic, extended(): value = jnp.concatenate([before, value, after], axis=dim)  26.5 us
    pallas_call x1, Pallas kernels, pressure_modes(): call(first_kernel, (big, strip, ends), 'first_solve')  18.7 us
    ppermute x8, starting transfers between devices, extended(): after = lax.ppermute(first, axis, down)  18.6 us
  transfers between devices with their start and end apart: 18, of which 0 were waited for; matrix products, arithmetic and copies ran while one was open for 39% of the time, Pallas kernels for 1%

profile of v1, /device:TPU:0, one launch (start us, length us, event | category | flops | bytes accessed | tf_op | source)
XLA Modules:
  0.0 453.7 jit_solution(882137976190283905)
XLA Ops:
  17.6 4.6 %copy.168 = f32[8,256,512]{2,0,1:T(8,128)S(1)} copy(f32[8,256,512]{2,1,0:T(8,128)} %param.29) | data formatting | bytes 8388608 | tf_op args[3]
  22.9 3.9 fusion.151
  27.6 8.5 %subtract_multiply_fusion = (f32[8,256,512]{2,0,1:T(8,128)}, f32[8,256,512]{2,0,1:T(8,128)S(1)}) fusion(f32[8,256,512]{2,0,1:T(8,128)S(1)} %copy.168, f32[2,256,512]{2,0,1:T(2,128)S(1)} %reshape.753, f32[3,256,512]{2,0,1:T(4,128)S(1)} %reshape.752, f32[8]{0:T(128)S(1)} %get-tuple-element.89, f32[8,256,512]{2,1,0:T(8,128)S(1)} %copy-done.17), kind=kLoop, calls=%fused_computation.104 | loop fusion | flops 27262976 | bytes 19398688 | tf_op jit(solution)/shard_map/mul | solution.py:50
  44.9 4.4 vertical_modes.1
  53.9 9.8 %subtract_multiply_fusion.1 = f32[8,256,512]{2,0,1:T(8,128)} fusion(f32[8,256,512]{2,0,1:T(8,128)S(1)} %copy-done.7, f32[1,256,512]{2,0,1:T(1,128)S(1)} %slice.537, f32[7,256,512]{2,0,1:T(8,128)} %slice.536, f32[2,256,512]{2,0,1:T(2,128)S(1)} %reshape.744, f32[3,256,512]{2,0,1:T(4,128)S(1)} %reshape.743, f32[8]{0:T(128)S(1)} %get-tuple-element.90), kind=kLoop, calls=%fused_computation.109 | loop fusion | flops 30408704 | bytes 15204384 | tf_op jit(solution)/shard_map/mul | solution.py:50
  64.3 4.4 copy.145
  68.7 4.4 copy.184
  94.3 23.3 %multiply_subtract_fusion = f32[8,256,513]{2,0,1:T(8,128)} fusion(f32[8,256,512]{2,0,1:T(8,128)} %copy.184, f32[8,256,3]{2,0,1:T(8,128)S(1)} %copy.137, f32[8,256,512]{2,0,1:T(8,128)} %copy-done.9, f32[8,256,3]{2,0,1:T(8,128)} %copy.187, f32[8,256,3]{2,0,1:T(8,128)} %copy.191), kind=kLoop, calls=%fused_computation.53 | loop fusion | flops 28366848 | bytes 12664832 | tf_op jit(solution)/shard_map/sub | solution.py:43
  137.7 14.6 %multiply_subtract_fusion.1 = f32[8,256,513]{2,0,1:T(8,128)} fusion(f32[1,262,518]{2,0,1:T(1,128)S(1)} %slice.513, f32[7,262,518]{2,0,1:T(8,128)S(1)} %slice.512, f32[8,262,518]{2,0,1:T(8,128)S(1)} %pad_maximum_fusion, f32[8,256,512]{2,0,1:T(8,128)S(1)} %copy-done.8, f32[8,256,3]{2,0,1:T(8,128)S(1)} %copy.151, f32[8,256,3]{2,0,1:T(8,128)S(1)} %copy.155), kind=kLoop, calls=%fused_computation.54 | loop fusion | flops 30468096 | bytes 16991360 | tf_op jit(solution)/shard_map/sub | solution.py:43
  155.9 4.0 maximum_maximum_fusion
  159.9 7.3 %maximum_maximum_fusion.2 = (f32[8,259,518]{2,0,1:T(8,128)}, f32[8,259,518]{2,0,1:T(8,128)}) fusion(f32[8,256,3]{2,0,1:T(8,128)S(1)} %copy-done.24, f32[8,256,512]{2,0,1:T(8,128)S(1)} %copy-done.12, f32[8,256,3]{2,0,1:T(8,128)S(1)} %copy-done.22, f32[8,3,518]{2,0,1:T(8,128)S(1)} %collective-permute-done.16, f32[8,3,518]{2,0,1:T(8,128)S(1)} %collective-permute-done.17), kind=kLoop, calls=%fused_computation.33 | loop fusion | flops 6439776 | bytes 12929280 | tf_op jit(solution)/shard_map/concatenate | solution.py:30
  167.2 17.5 %multiply_subtract_fusion.2 = f32[8,257,512]{2,0,1:T(8,128)} fusion(f32[8,259,518]{2,0,1:T(8,128)} %maximum_maximum_fusion, f32[8,259,518]{2,0,1:T(8,128)} %get-tuple-element.47, f32[8,259,518]{2,0,1:T(8,128)} %get-tuple-element.46), kind=kLoop, calls=%fused_computation.58 | loop fusion | flops 21053440 | bytes 33685504 | tf_op jit(solution)/shard_map/sub | solution.py:43
  184.7 3.7 pad_maximum_fusion.1
  193.0 7.1 %maximum_maximum_fusion.1 = (f32[8,259,518]{2,0,1:T(8,128)}, f32[8,259,518]{2,0,1:T(8,128)}) fusion(f32[8,256,3]{2,0,1:T(8,128)S(1)} %copy.155, f32[8,256,512]{2,0,1:T(8,128)S(1)} %copy-done.8, f32[8,256,3]{2,0,1:T(8,128)S(1)} %copy.151, f32[8,3,518]{2,0,1:T(8,128)S(1)} %collective-permute-done.10, f32[8,3,518]{2,0,1:T(8,128)S(1)} %collective-permute-done.11), kind=kLoop, calls=%fused_computation.31 | loop fusion | flops 6439776 | bytes 12929280 | tf_op jit(solution)/shard_map/concatenate | solution.py:30
  200.2 20.6 %multiply_subtract_fusion.3 = f32[8,257,512]{2,0,1:T(8,128)} fusion(f32[1,262,518]{2,0,1:T(1,128)S(1)} %slice.526, f32[7,262,518]{2,0,1:T(8,128)} %slice.525, f32[8,262,518]{2,0,1:T(8,128)} %copy-done.15, f32[8,259,518]{2,0,1:T(8,128)} %get-tuple-element.53, f32[8,259,518]{2,0,1:T(8,128)} %get-tuple-element.52), kind=kLoop, calls=%fused_computation.59 | loop fusion | flops 24211456 | bytes 38028416 | tf_op jit(solution)/shard_map/sub | solution.py:43
  220.9 30.3 %broadcast_multiply_fusion = (f32[8,256,512]{2,0,1:T(8,128)S(1)}, f32[8,256,512]{2,0,1:T(8,128)}, f32[8,256,512]{2,0,1:T(8,128)}) fusion(f32[8]{0:T(128)S(1)} %copy-done.49, f32[1,256,512]{2,0,1:T(1,128)S(1)} %copy-done.30, f32[7,256,512]{2,0,1:T(8,128)} %slice.545, f32[8,256,512]{2,1,0:T(8,128)} %param.29, f32[8]{0:T(128)S(1)} %copy-done.74, ...), kind=kLoop, calls=%fused_computation.113 | loop fusion | flops 26214400 | bytes 74448992 | tf_op jit(solution)/shard_map/mul | solution.py:411
  251.2 13.6 %fusion.45.modes_ref = f32[2048,512]{1,0:T(8,128)} fusion(f32[8,256,512]{2,0,1:T(8,128)S(1)} %copy-done.14, f32[8,256,3]{2,0,1:T(8,128)S(1)} %copy.137, f32[8,259,518]{2,0,1:T(8,128)} %maximum_maximum_fusion, f32[8,256,512]{2,0,1:T(8,128)S(1)} %get-tuple-element.38, f32[7,256,512]{2,0,1:T(8,128)S(1)} %bitcast.116, f32[8]{0:T(128)S(1)} %copy-done.60, ...), kind=kOutput, calls=%fused_computation.110 | convolution fusion | flops 109051968 | bytes 24666432 | tf_op jit(solution)/shard_map/kl,lyx->ykx/dot_general | solution.py:420
  264.9 18.7 %first_solve.1 = (f32[2048,512]{1,0:T(8,128)}, f32[2048,128]{1,0:T(8,128)S(1)}, f32[2,8,512]{2,1,0:T(8,128)S(1)}) custom-call(f32[2048,512]{1,0:T(8,128)} %fusion.45.modes_ref, f32[512,512]{1,0:T(8,128)S(1)} %copy-done.1, f32[512,128]{1,0:T(8,128)S(1)} %copy-done.2, f32[8,512]{1,0:T(8,128)S(1)} %get-tuple-element.84.decay_ref, ...), custom_call_target="tpu_custom_call" | custom-call | tf_op jit(solution)/shard_map/first_solve/pallas_call | solution.py:368
  283.5 14.3 %all-gather = f32[16,8,512]{2,1,0:T(8,128)S(1)} all-gather(f32[2,8,512]{2,1,0:T(8,128)S(1)} %get-tuple-element.15), channel_id=2, replica_groups=mesh['gx'=4,'gy'=8] {'gy'}, dimensions={0}, use_global_device_ids=true | all-gather | bytes 294912 | tf_op jit(solution)/shard_map/all_gather | solution.py:262
  298.2 7.1 %edge_terms.1 = f32[2048,128]{1,0:T(8,128)S(1)} custom-call(f32[8,512]{1,0:T(8,128)S(1)} %get-tuple-element.84.decay_ref, f32[2,8,512]{2,1,0:T(8,128)S(1)} %pad_maximum_fusion.29.ends_ref, f32[512,128]{1,0:T(8,128)S(1)} %copy-done.2, f32[2048,128]{1,0:T(8,128)S(1)} %get-tuple-element.16.edge_in_ref), custom_call_target="tpu_custom_call" | custom-call | tf_op jit(solution)/shard_map/edge_terms/pallas_call | solution.py:371
  305.7 40.0 %all-gather.1 = f32[64,8,256]{2,1,0:T(8,128)S(1)} all-gather(f32[2,8,256]{2,1,0:T(8,128)S(1)} %bitcast.129), channel_id=3, replica_groups=mesh['gx'=4,'gy'=8] {'gx','gy'}, dimensions={0}, use_global_device_ids=true | all-gather | bytes 540672 | tf_op jit(solution)/shard_map/all_gather | solution.py:323
  355.5 8.7 %second_solve.1 = (f32[2048,512]{1,0:T(8,128)S(1)}, f32[2,8,512]{2,1,0:T(8,128)S(1)}) custom-call(f32[2048,512]{1,0:T(8,128)} %get-tuple-element.14.spectral_ref, f32[2048,128]{1,0:T(8,128)S(1)} %pad.8.line_ref, f32[128,512]{1,0:T(8,128)S(1)} %copy-done.3, f32[8,512]{1,0:T(8,128)S(1)} %get-tuple-element.84.decay_ref, f32[8,512]{1,0:T(8,128)S(1)} %get-tuple-element.83.start_ref), custom_call_target="tpu_custom_call" | custom-call | tf_op jit(solution)/shard_map/second_solve/pallas_call | solution.py:373
  366.2 14.4 %all-gather.2 = f32[16,8,512]{2,1,0:T(8,128)S(1)} all-gather(f32[2,8,512]{2,1,0:T(8,128)S(1)} %get-tuple-element.18), channel_id=4, replica_groups=mesh['gx'=4,'gy'=8] {'gy'}, dimensions={0}, use_global_device_ids=true | all-gather | bytes 294912 | tf_op jit(solution)/shard_map/all_gather | solution.py:262
  380.9 15.0 %to_columns.1 = f32[2048,512]{1,0:T(8,128)} custom-call(f32[2048,512]{1,0:T(8,128)} %copy-done, f32[2048,128]{1,0:T(8,128)S(1)} %pad.8.line_ref, f32[512,512]{1,0:T(8,128)S(1)} %copy-done.1, f32[8,512]{1,0:T(8,128)S(1)} %get-tuple-element.84.decay_ref, f32[2,8,512]{2,1,0:T(8,128)S(1)} %pad_maximum_fusion.30.ends_ref), custom_call_target="tpu_custom_call" | custom-call | tf_op jit(solution)/shard_map/to_columns/pallas_call | solution.py:376
  395.9 5.8 %fusion.40 = f32[8,256,512]{2,0,1:T(8,128)S(1)} fusion(f32[8,8,1]{1,0,2:T(8,128)S(1)} %copy-done.43, f32[2048,512]{1,0:T(8,128)} %to_columns.1), kind=kOutput, calls=%fused_computation.102 | convolution fusion | flops 100663296 | bytes 8388864 | tf_op jit(solution)/shard_map/kl,ykx->lyx/dot_general | solution.py:422
  404.3 5.5 %slice.562 = f32[8,256,511]{2,0,1:T(8,128)} slice(f32[8,256,512]{2,0,1:T(8,128)} %copy-done.4), slice={[0:8], [0:256], [1:512]} | slice | bytes 8372224 | tf_op jit(solution)/shard_map/slice | solution.py:382
  414.8 4.4 copy.206
  419.3 4.4 copy.205
  425.1 15.0 %divide_subtract_fusion = (f32[8,256,512]{2,0,1:T(8,128)S(1)}, f32[8,256,512]{2,0,1:T(8,128)S(1)}, f32[8,256,512]{2,0,1:T(8,128)S(1)}) fusion(f32[8,256,512]{2,0,1:T(8,128)} %get-tuple-element.39, f32[8,256,512]{2,0,1:T(8,128)} %copy-done.4, f32[7,256,512]{2,0,1:T(8,128)} %slice.566, f32[8]{0:T(128)S(1)} %copy-done.58, ...), kind=kLoop, calls=%fused_computation.105 | loop fusion | flops 12582912 | bytes 41418784 | tf_op jit(solution)/shard_map/sub | solution.py:427
  440.1 4.4 copy.202
  444.5 4.4 copy.203
  449.0 4.4 copy.204
  (286 shorter events, 102.9 us)
Async XLA Ops:
  2.9 76.4 %collective-permute-start.7 = (f32[8,256,3]{1,0,2:T(8,128)S(1)}, f32[8,256,3]{1,0,2:T(8,128)S(1)}, u32[]{:S(2)}, u32[]{:S(2)}) collective-permute-start(f32[8,256,3]{1,0,2:T(8,128)S(1)} %copy.218), channel_id=1, source_target_pairs={{0,8},{8,16},{16,24},{24,0},{1,9},{9,17},{17,25},{25,1},{2,10},{10... | collective-permute-start | bytes 73736 | tf_op jit(solution)/shard_map/ppermute | solution.py:28
  6.2 76.4 %collective-permute-start.8 = (f32[8,256,3]{1,0,2:T(8,128)S(1)}, f32[8,256,3]{1,0,2:T(8,128)S(1)}, u32[]{:S(2)}, u32[]{:S(2)}) collective-permute-start(f32[8,256,3]{1,0,2:T(8,128)S(1)} %copy.219), channel_id=1, source_target_pairs={{8,0},{16,8},{24,16},{0,24},{9,1},{17,9},{25,17},{1,25},{10,2},{18... | collective-permute-start | bytes 73736 | tf_op jit(solution)/shard_map/ppermute | solution.py:29
  10.0 111.3 %collective-permute-start.1 = (f32[8,256,3]{1,0,2:T(8,128)}, f32[8,256,3]{1,0,2:T(8,128)S(1)}, u32[]{:S(2)}, u32[]{:S(2)}) collective-permute-start(f32[8,256,3]{1,0,2:T(8,128)} %copy.215), channel_id=1, source_target_pairs={{0,8},{8,16},{16,24},{24,0},{1,9},{9,17},{17,25},{25,1},{2,10},{10... | collective-permute-start | bytes 73736 | tf_op jit(solution)/shard_map/ppermute | solution.py:28
  11.4 114.8 %collective-permute-start.2 = (f32[8,256,3]{1,0,2:T(8,128)S(1)}, f32[8,256,3]{1,0,2:T(8,128)S(1)}, u32[]{:S(2)}, u32[]{:S(2)}) collective-permute-start(f32[8,256,3]{1,0,2:T(8,128)S(1)} %copy.216), channel_id=1, source_target_pairs={{8,0},{16,8},{24,16},{0,24},{9,1},{17,9},{25,17},{1,25},{10,2},{18... | collective-permute-start | bytes 73736 | tf_op jit(solution)/shard_map/ppermute | solution.py:29
  15.5 69.2 %collective-permute-start = (f32[8,256,3]{1,0,2:T(8,128)S(1)}, f32[8,256,3]{1,0,2:T(8,128)S(1)}, u32[]{:S(2)}, u32[]{:S(2)}) collective-permute-start(f32[8,256,3]{1,0,2:T(8,128)S(1)} %copy.214), channel_id=1, source_target_pairs={{0,8},{8,16},{16,24},{24,0},{1,9},{9,17},{17,25},{25,1},{2,10},{10... | collective-permute-start | bytes 73736 | tf_op jit(solution)/shard_map/ppermute | solution.py:28
  50.3 247.7 %copy-start.46 = (f32[8]{0:T(128)}, f32[8]{0:T(128)S(1)}, u32[]{:S(2)}) copy-start(f32[8]{0:T(128)S(1)} %slice_reduce_fusion.1) | copy-start | bytes 100
  79.2 7.4 %collective-permute-start.14 = (f32[8,256,3]{1,0,2:T(8,128)}, f32[8,256,3]{1,0,2:T(8,128)S(1)}, u32[]{:S(2)}, u32[]{:S(2)}) collective-permute-start(f32[8,256,3]{1,0,2:T(8,128)} %copy.224), channel_id=1, source_target_pairs={{0,8},{8,16},{16,24},{24,0},{1,9},{9,17},{17,25},{25,1},{2,10},{10... | collective-permute-start | bytes 73736 | tf_op jit(solution)/shard_map/ppermute | solution.py:28
  82.6 5.5 %collective-permute-start.15 = (f32[8,256,3]{1,0,2:T(8,128)S(1)}, f32[8,256,3]{1,0,2:T(8,128)S(1)}, u32[]{:S(2)}, u32[]{:S(2)}) collective-permute-start(f32[8,256,3]{1,0,2:T(8,128)S(1)} %copy.225), channel_id=1, source_target_pairs={{8,0},{16,8},{24,16},{0,24},{9,1},{17,9},{25,17},{1,25},{10,2},{18... | collective-permute-start | bytes 73736 | tf_op jit(solution)/shard_map/ppermute | solution.py:29
  84.7 33.6 %collective-permute-start.4 = (f32[8,256,3]{1,0,2:T(8,128)S(1)}, f32[8,256,3]{1,0,2:T(8,128)S(1)}, u32[]{:S(2)}, u32[]{:S(2)}) collective-permute-start(f32[8,256,3]{1,0,2:T(8,128)S(1)} %copy.217), channel_id=1, source_target_pairs={{8,0},{16,8},{24,16},{0,24},{9,1},{17,9},{25,17},{1,25},{10,2},{18... | collective-permute-start | bytes 73736 | tf_op jit(solution)/shard_map/ppermute | solution.py:29
  86.6 106.4 %collective-permute-start.10 = (f32[8,3,518]{2,0,1:T(8,128)}, f32[8,3,518]{2,0,1:T(8,128)S(1)}, u32[]{:S(2)}, u32[]{:S(2)}) collective-permute-start(f32[8,3,518]{2,0,1:T(8,128)} %get-tuple-element.54), channel_id=1, source_target_pairs={{0,1},{1,2},{2,3},{3,4},{4,5},{5,6},{6,7},{7,0},{8,9},{9,10},{10,1... | collective-permute-start | bytes 149192 | tf_op jit(solution)/shard_map/ppermute | solution.py:28
  88.7 104.4 %collective-permute-start.11 = (f32[8,3,518]{2,0,1:T(8,128)}, f32[8,3,518]{2,0,1:T(8,128)S(1)}, u32[]{:S(2)}, u32[]{:S(2)}) collective-permute-start(f32[8,3,518]{2,0,1:T(8,128)} %get-tuple-element.55), channel_id=1, source_target_pairs={{1,0},{2,1},{3,2},{4,3},{5,4},{6,5},{7,6},{0,7},{9,8},{10,9},{11,1... | collective-permute-start | bytes 149192 | tf_op jit(solution)/shard_map/ppermute | solution.py:29
  121.3 8.1 %collective-permute-start.5 = (f32[8,3,518]{2,0,1:T(8,128)}, f32[8,3,518]{2,0,1:T(8,128)S(1)}, u32[]{:S(2)}, u32[]{:S(2)}) collective-permute-start(f32[8,3,518]{2,0,1:T(8,128)} %get-tuple-element.50), channel_id=1, source_target_pairs={{0,1},{1,2},{2,3},{3,4},{4,5},{5,6},{6,7},{7,0},{8,9},{9,10},{10,1... | collective-permute-start | bytes 149192 | tf_op jit(solution)/shard_map/ppermute | solution.py:28
  121.3 11.6 %collective-permute-start.6 = (f32[8,3,518]{2,0,1:T(8,128)S(1)}, f32[8,3,518]{2,0,1:T(8,128)}, u32[]{:S(2)}, u32[]{:S(2)}) collective-permute-start(f32[8,3,518]{2,0,1:T(8,128)S(1)} %get-tuple-element.51), channel_id=1, source_target_pairs={{1,0},{2,1},{3,2},{4,3},{5,4},{6,5},{7,6},{0,7},{9,8},{10,9},{11,1... | collective-permute-start | bytes 149192 | tf_op jit(solution)/shard_map/ppermute | solution.py:29
  129.3 23.0 %collective-permute-start.3 = (f32[8,3,518]{2,0,1:T(8,128)S(1)}, f32[8,3,518]{2,0,1:T(8,128)S(1)}, u32[]{:S(2)}, u32[]{:S(2)}) collective-permute-start(f32[8,3,518]{2,0,1:T(8,128)S(1)} %get-tuple-element.57), channel_id=1, source_target_pairs={{0,1},{1,2},{2,3},{3,4},{4,5},{5,6},{6,7},{7,0},{8,9},{9,10},{10,1... | collective-permute-start | bytes 149192 | tf_op jit(solution)/shard_map/ppermute | solution.py:28
  129.3 55.3 %collective-permute-start.9 = (f32[8,3,518]{2,0,1:T(8,128)}, f32[8,3,518]{2,0,1:T(8,128)}, u32[]{:S(2)}, u32[]{:S(2)}) collective-permute-start(f32[8,3,518]{2,0,1:T(8,128)} %get-tuple-element.56), channel_id=1, source_target_pairs={{1,0},{2,1},{3,2},{4,3},{5,4},{6,5},{7,6},{0,7},{9,8},{10,9},{11,1... | collective-permute-start | bytes 149192 | tf_op jit(solution)/shard_map/ppermute | solution.py:29
  132.9 27.0 %collective-permute-start.16 = (f32[8,3,518]{2,0,1:T(8,128)}, f32[8,3,518]{2,0,1:T(8,128)S(1)}, u32[]{:S(2)}, u32[]{:S(2)}) collective-permute-start(f32[8,3,518]{2,0,1:T(8,128)} %get-tuple-element.48), channel_id=1, source_target_pairs={{0,1},{1,2},{2,3},{3,4},{4,5},{5,6},{6,7},{7,0},{8,9},{9,10},{10,1... | collective-permute-start | bytes 149192 | tf_op jit(solution)/shard_map/ppermute | solution.py:28
  152.3 7.6 %collective-permute-start.17 = (f32[8,3,518]{2,0,1:T(8,128)S(1)}, f32[8,3,518]{2,0,1:T(8,128)S(1)}, u32[]{:S(2)}, u32[]{:S(2)}) collective-permute-start(f32[8,3,518]{2,0,1:T(8,128)S(1)} %copy-done.33), channel_id=1, source_target_pairs={{1,0},{2,1},{3,2},{4,3},{5,4},{6,5},{7,6},{0,7},{9,8},{10,9},{11,1... | collective-permute-start | bytes 149192 | tf_op jit(solution)/shard_map/ppermute | solution.py:29
  220.8 30.3 %copy-start.19 = (f32[8,256,512]{2,1,0:T(8,128)S(1)}, f32[8,256,512]{2,1,0:T(8,128)}, u32[]{:S(2)}) copy-start(f32[8,256,512]{2,1,0:T(8,128)} %param.27) | copy-start | bytes 12582916
  220.8 30.3 %copy-start.61 = (f32[8,8]{1,0:T(8,128)S(1)}, f32[8,8]{1,0:T(8,128)}, u32[]{:S(2)}) copy-start(f32[8,8]{1,0:T(8,128)} %get-tuple-element.74) | copy-start | bytes 772
  220.8 30.3 %copy-start.73 = (f32[8]{0:T(128)S(1)}, f32[8]{0:T(128)}, u32[]{:S(2)}) copy-start(f32[8]{0:T(128)} %copy-done.72) | copy-start | bytes 100
  264.8 33.0 %copy-start.53 = (pred[8]{0:T(512)(128)(4,1)S(1)}, pred[8]{0:T(512)(128)(4,1)}, u32[]{:S(2)}) copy-start(pred[8]{0:T(512)(128)(4,1)} %get-tuple-element.93) | copy-start | bytes 28
  264.8 33.0 %copy-start.55 = (pred[8]{0:T(512)(128)(4,1)S(1)}, pred[8]{0:T(512)(128)(4,1)}, u32[]{:S(2)}) copy-start(pred[8]{0:T(512)(128)(4,1)} %get-tuple-element.94) | copy-start | bytes 28
  264.8 33.0 %copy-start.64 = (pred[8]{0:T(512)(128)(4,1)S(1)}, pred[8]{0:T(512)(128)(4,1)}, u32[]{:S(2)}) copy-start(pred[8]{0:T(512)(128)(4,1)} %get-tuple-element.95) | copy-start | bytes 28
  264.8 33.0 %copy-start.66 = (pred[8]{0:T(512)(128)(4,1)S(1)}, pred[8]{0:T(512)(128)(4,1)}, u32[]{:S(2)}) copy-start(pred[8]{0:T(512)(128)(4,1)} %get-tuple-element.96) | copy-start | bytes 28
  264.8 33.0 %copy-start.68 = (pred[8]{0:T(512)(128)(4,1)S(1)}, pred[8]{0:T(512)(128)(4,1)}, u32[]{:S(2)}) copy-start(pred[8]{0:T(512)(128)(4,1)} %get-tuple-element.91) | copy-start | bytes 28
  264.8 33.0 %copy-start.70 = (pred[8]{0:T(512)(128)(4,1)S(1)}, pred[8]{0:T(512)(128)(4,1)}, u32[]{:S(2)}) copy-start(pred[8]{0:T(512)(128)(4,1)} %get-tuple-element.92) | copy-start | bytes 28
  264.8 33.2 %copy-start.51 = (pred[512]{0:T(512)(128)(4,1)S(1)}, pred[512]{0:T(512)(128)(4,1)}, u32[]{:S(2)}) copy-start(pred[512]{0:T(512)(128)(4,1)} %constant.186) | copy-start | bytes 1540
  305.7 43.4 %copy-start.36 = (f32[64,64,1]{1,0,2:T(8,128)S(1)}, f32[64,64,1]{1,0,2:T(8,128)}, u32[]{:S(2)}) copy-start(f32[64,64,1]{1,0,2:T(8,128)} %constant.188) | copy-start | bytes 49156
  355.4 25.4 %copy-start.39 = (f32[512]{0:T(512)S(1)}, f32[512]{0:T(512)}, u32[]{:S(2)}) copy-start(f32[512]{0:T(512)} %constant.160.clone) | copy-start | bytes 6148
  355.4 25.4 %copy-start.52 = (pred[512]{0:T(512)(128)(4,1)S(1)}, pred[512]{0:T(512)(128)(4,1)}, u32[]{:S(2)}) copy-start(pred[512]{0:T(512)(128)(4,1)} %constant.186) | copy-start | bytes 1540
  401.7 23.3 %collective-permute-start.13 = (f32[8,1,512]{2,0,1:T(8,128)S(1)}, f32[8,1,512]{2,0,1:T(8,128)S(1)}, u32[]{:S(2)}, u32[]{:S(2)}) collective-permute-start(f32[8,1,512]{2,0,1:T(8,128)S(1)} %slice.565), channel_id=1, source_target_pairs={{0,7},{1,0},{2,1},{3,2},{4,3},{5,4},{6,5},{7,6},{8,15},{9,8},{10,9... | collective-permute-start | bytes 49160 | tf_op jit(solution)/shard_map/ppermute | solution.py:18
  404.2 19.5 %collective-permute-start.12 = (f32[8,256,1]{1,0,2:T(8,128)S(1)}, f32[8,256,1]{1,0,2:T(8,128)S(1)}, u32[]{:S(2)}, u32[]{:S(2)}) collective-permute-start(f32[8,256,1]{1,0,2:T(8,128)S(1)} %copy.182), channel_id=1, source_target_pairs={{0,24},{8,0},{16,8},{24,16},{1,25},{9,1},{17,9},{25,17},{2,26},{10... | collective-permute-start | bytes 24584 | tf_op jit(solution)/shard_map/ppermute | solution.py:18
  (63 other events, 697.7 us)

commit v2 on v1

--- a/solution.py
+++ b/solution.py
@@ -18,48 +18,8 @@
     return lax.ppermute(value, axis, pairs)
 
 
-def extended(value, sides, width):
-    for axis, dim in sides:
-        size, length = (lax.axis_size(axis), value.shape[dim])
-        up = [(i, (i + 1) % size) for i in range(size)]
-        down = [(j, i) for i, j in up]
-        last = lax.slice_in_dim(value, length - width, length, axis=dim)
-        first = lax.slice_in_dim(value, 0, width, axis=dim)
-        before = lax.ppermute(last, axis, up)
-        after = lax.ppermute(first, axis, down)
-        value = jnp.concatenate([before, value, after], axis=dim)
-    return value
-
-
 def lift_level(field):
     return jnp.concatenate([field[1:], field[-1:]], axis=0)
-
-
-def upwind_flux(q_m2, q_m1, q_zero, q_p1, q_p2, q_p3, velocity):
-    centred = velocity * (37.0 * (q_zero + q_p1) - 8.0 * (q_m1 + q_p2) + (q_m2 + q_p3)) / 60.0
-    damped = (
-        jnp.abs(velocity) * (10.0 * (q_p1 - q_zero) - 5.0 * (q_p2 - q_m1) + (q_p3 - q_m2)) / 60.0
-    )
-    return centred - damped
-
-
-def vertical_tend(tracer, velocity, rho_face, rho_level, spacing):
-    levels = tracer.shape[0]
-    padded = jnp.pad(tracer, ((2, 3), (0, 0), (0, 0)), mode="edge")
-    parts = [padded[2 + offset : 2 + offset + levels] for offset in range(-2, 4)]
-    flux_z = upwind_flux(*parts, velocity) * rho_face[:, None, None]
-    below = jnp.concatenate([jnp.zeros_like(flux_z[:1]), flux_z[:-1]], axis=0)
-    return -(flux_z - below) / (rho_level * spacing)[:, None, None]
-
-
-def horizontal_local(tracer_rim, u_rim, v_rim, rows_y, cols_x):
-    row_band = tracer_rim[:, 3 : 3 + rows_y, :]
-    parts_x = [row_band[:, :, 2 + offset : 3 + offset + cols_x] for offset in range(-2, 4)]
-    flux_x = upwind_flux(*parts_x, u_rim[:, 3 : 3 + rows_y, 2 : 3 + cols_x])
-    col_band = tracer_rim[:, :, 3 : 3 + cols_x]
-    parts_y = [col_band[:, 2 + offset : 3 + offset + rows_y, :] for offset in range(-2, 4)]
-    flux_y = upwind_flux(*parts_y, v_rim[:, 2 : 3 + rows_y, 3 : 3 + cols_x])
-    return -(flux_x[:, :, 1:] - flux_x[:, :, :-1]) - (flux_y[:, 1:, :] - flux_y[:, :-1, :])
 
 
 high = lax.Precision.HIGHEST
@@ -151,48 +111,34 @@
     return weights
 
 
-def run_sweeps(source, decay_ref, start_ref, work_ref, ends_ref, rows, levels):
-    decay = decay_ref[...]
-
-    def forward(j, carry):
-        at = pl.ds(pl.multiple_of(j * levels, levels), levels)
-        value = carry + source(at)
-        scaled = decay * value
-        work_ref[at, :] = scaled
+def row_of(j, levels):
+    return pl.ds(pl.multiple_of(j * levels, levels), levels)
+
+
+def forward_rows(source, decay, work_ref, first, rows, carry):
+    levels = decay.shape[0]
+
+    def step(j, carry):
+        scaled = decay * (carry + source(j))
+        work_ref[row_of(first + j, levels), :] = scaled
         return scaled
 
-    last = lax.fori_loop(0, rows, forward, jnp.zeros_like(decay), unroll=4)
-    top = start_ref[...] * last
+    return lax.fori_loop(0, rows, step, carry, unroll=4)
+
+
+def backward_rows(last, decay, start, work_ref, ends_ref, rows):
+    levels = decay.shape[0]
+    top = start * last
     ends_ref[0] = top
-    work_ref[pl.ds((rows - 1) * levels, levels), :] = top
-
-    def backward(step, carry):
-        at = pl.ds(pl.multiple_of((rows - 2 - step) * levels, levels), levels)
+    work_ref[row_of(rows - 1, levels), :] = top
+
+    def step(j, carry):
+        at = row_of(rows - 2 - j, levels)
         value = decay * carry - work_ref[at, :]
         work_ref[at, :] = value
         return value
 
-    ends_ref[1] = lax.fori_loop(0, rows - 1, backward, top, unroll=4)
-
-
-def first_kernel(modes_ref, sine_ref, weight_ref, decay_ref, start_ref, spectral_ref, edge_ref, ends_ref, work_ref):
-    total, count = modes_ref.shape
-    levels = decay_ref.shape[0]
-    chunk = min(256, total)
-
-    @pl.loop(0, total // chunk)
-    def _(step):
-        at = pl.ds(pl.multiple_of(step * chunk, chunk), chunk)
-        spectral_ref[at, :] = jnp.dot(modes_ref[at, :], sine_ref[...], precision=high)
-
-    run_sweeps(lambda at: spectral_ref[at, :], decay_ref, start_ref, work_ref, ends_ref, total // levels, levels)
-
-    @pl.loop(0, total // chunk)
-    def _(step):
-        at = pl.ds(pl.multiple_of(step * chunk, chunk), chunk)
-        lane = lax.broadcasted_iota(jnp.int32, (chunk, 128), 1)
-        near = jnp.where(lane == 0, spectral_ref[at, 0:128], 0.0)
-        edge_ref[at, :] = near - jnp.dot(work_ref[at, :], weight_ref[...], precision=high)
+    ends_ref[1] = lax.fori_loop(0, rows - 1, step, top, unroll=4)
 
 
 def coupled_terms(decay_ref, ends_ref, work_ref, rows, levels):
@@ -238,23 +184,11 @@
         at = pl.ds(pl.multiple_of(step * chunk, chunk), chunk)
         work_ref[at, :] = spectral_ref[at, :] - jnp.dot(line_ref[at, :], spread_ref[...], precision=high)
 
-    run_sweeps(lambda at: work_ref[at, :], decay_ref, start_ref, free_ref, ends_ref, total // levels, levels)
-
-
-def fourth_kernel(free_ref, line_ref, sine_ref, decay_ref, ends_ref, out_ref, work_ref):
-    total, count = free_ref.shape
-    levels = decay_ref.shape[0]
-    chunk = min(256, total)
-    work_ref[...] = free_ref[...]
-    coupled_terms(decay_ref, ends_ref, work_ref, total // levels, levels)
-
-    @pl.loop(0, total // chunk)
-    def _(step):
-        at = pl.ds(pl.multiple_of(step * chunk, chunk), chunk)
-        lane = lax.broadcasted_iota(jnp.int32, (chunk, count), 1)
-        column = jnp.broadcast_to(line_ref[at, 0:1], (chunk, count))
-        full = jnp.where(lane == 0, column, work_ref[at, :])
-        out_ref[at, :] = jnp.dot(full, sine_ref[...], precision=high)
+    decay, rows = decay_ref[...], total // levels
+    last = forward_rows(
+        lambda j: work_ref[row_of(j, levels), :], decay, free_ref, 0, rows, jnp.zeros_like(decay)
+    )
+    backward_rows(last, decay, start_ref[...], free_ref, ends_ref, rows)
 
 
 def couple(ends, ratio):
@@ -340,91 +274,434 @@
     east = sum((powers[d] + powers[groups_x - d]) * ahead[d + 1] for d in range(groups_x))
     solved = jnp.stack([own * scale, east * scale]).reshape(2 * levels, outer, inner)
     whole = hartley_back(solved).reshape(2, levels, count)
-    mine = lax.dynamic_slice_in_dim(whole, lax.axis_index("gy") * rows, rows, axis=2)
-    flat = mine.transpose(2, 1, 0).reshape(rows * levels, 2)
+    whole = jnp.concatenate([whole, whole[:, :, :1]], axis=2)
+    mine = lax.dynamic_slice_in_dim(whole, lax.axis_index("gy") * rows, rows + 1, axis=2)
+    flat = mine.transpose(2, 1, 0).reshape((rows + 1) * levels, 2)
     return jnp.pad(flat, ((0, 0), (0, 126)))
 
 
-def pressure_modes(modes, square):
-    total, cols_x = modes.shape
-    levels = square.shape[0]
-    rows = total // levels
-    sine = sine_matrix(cols_x)
-    weight = edge_weights(cols_x)
-    index = np.arange(cols_x)
-    excess = (4.0 * np.sin(np.pi * index / (2 * cols_x)) ** 2).astype(np.float32) + square[:, None]
+def upper_of(field):
+    rolled = pltpu.roll(field, field.shape[0] - 1, 0)
+    sub = lax.broadcasted_iota(jnp.int32, field.shape, 0)
+    return jnp.where(sub == field.shape[0] - 1, field, rolled)
+
+
+def lower_of(field):
+    rolled = pltpu.roll(field, 1, 0)
+    sub = lax.broadcasted_iota(jnp.int32, field.shape, 0)
+    return jnp.where(sub == 0, field, rolled)
+
+
+def zero_below(field):
+    sub = lax.broadcasted_iota(jnp.int32, field.shape, 0)
+    return jnp.where(sub == 0, 0.0, pltpu.roll(field, 1, 0))
+
+
+def flux60(q_m2, q_m1, q_zero, q_p1, q_p2, q_p3, speed):
+    centred = 37.0 * (q_zero + q_p1) - 8.0 * (q_m1 + q_p2) + (q_m2 + q_p3)
+    damped = 10.0 * (q_p1 - q_zero) - 5.0 * (q_p2 - q_m1) + (q_p3 - q_m2)
+    return speed * centred - jnp.abs(speed) * damped
+
+
+def wide(tile, count):
+    return jnp.concatenate([tile] * (count // tile.shape[1]), axis=1)
+
+
+def mix_levels(field, mixer):
+    total = mixer[0] * field
+    for shift in range(1, field.shape[0]):
+        total = total + mixer[shift] * pltpu.roll(field, shift, 0)
+    return total
+
+
+def pack_kernel(
+    th_lo, th_hi, w_lo, w_hi, v_hi, th_left, th_right, w_left, w_right, u_right, north, south, east, west
+):
+    north[0] = jnp.concatenate([th_hi[0, 5:8], w_hi[0, 5:8], v_hi[0, 7:8], v_hi[0, 7:8]], axis=0)
+    south[0] = jnp.concatenate([th_lo[0, 0:3], w_lo[0, 0:3], w_lo[0, 0:2]], axis=0)
+    lane = lax.broadcasted_iota(jnp.int32, th_left.shape[1:], 1)
+    merged = jnp.where(lane < 3, pltpu.roll(th_right[0], 3, 1), pltpu.roll(w_right[0], 6, 1))
+    merged = jnp.where(lane < 6, merged, pltpu.roll(u_right[0], 7, 1))
+    east[0] = merged.T[0:8, :]
+    west[0] = jnp.where(lane < 3, th_left[0], pltpu.roll(w_left[0], 3, 1)).T[0:8, :]
+
+
+def pack_sides(u_face, v_face, w_face, theta_field):
+    levels, rows, cols = theta_field.shape
+    low = pl.BlockSpec((1, 8, cols), lambda k: (k, 0, 0))
+    top = pl.BlockSpec((1, 8, cols), lambda k: (k, rows // 8 - 1, 0))
+    left = pl.BlockSpec((1, rows, 128), lambda k: (k, 0, 0))
+    right = pl.BlockSpec((1, rows, 128), lambda k: (k, 0, cols // 128 - 1))
+    flat = jax.ShapeDtypeStruct((levels, 8, cols), jnp.float32)
+    tall = jax.ShapeDtypeStruct((levels, 8, rows), jnp.float32)
+    tall_spec = pl.BlockSpec((1, 8, rows), lambda k: (k, 0, 0))
+    return pl.pallas_call(
+        pack_kernel,
+        grid=(levels,),
+        in_specs=[low, top, low, top, top, left, right, left, right, right],
+        out_specs=(low, low, tall_spec, tall_spec),
+        out_shape=(flat, flat, tall, tall),
+        name="pack_sides",
+    )(theta_field, theta_field, w_face, w_face, v_face, theta_field, theta_field, w_face, w_face, u_face)
+
+
+def rim_lanes(west, east, own):
+    flux_theta = flux60(*[west[:, f] for f in range(3)], *[own[:, f] for f in range(3)], west[:, 6] * (time_step / 60.0))
+    u_sum = (west[:, 6] + lift_level(west[:, 6])) * (0.5 * time_step / 60.0)
+    flux_w = flux60(*[west[:, f] for f in range(3, 6)], *[own[:, f] for f in range(3, 6)], u_sum)
+    fields = jnp.concatenate(
+        [east[:, :6], flux_theta[:, None], flux_w[:, None], west[:, 6:7], west[:, :6]], axis=1
+    )
+    return jnp.pad(fields.transpose(2, 0, 1), ((0, 0), (0, 0), (0, 128 - fields.shape[1])))
+
+
+def advect_kernel(
+    th_ref, th_lo, th_hi, w_ref, w_lo, w_hi, u_ref, v_ref, south, north, rim_ref, coef_ref, mixer_ref,
+    sine_ref, weight_ref, decay_ref, start_ref,
+    theta_out, star_out, spectral_out, edge_out, ends_out,
+    th_s, w_s, u_s, v_s, new_s, modes_s, flow_s, carry_s, work_s,
+):
+    tile, tiles = pl.program_id(0), pl.num_programs(0)
+    levels, rows, cols = th_ref.shape
+    pairs = ((th_s, th_ref, th_lo, th_hi, 0), (w_s, w_ref, w_lo, w_hi, 3))
+
+    @pl.loop(0, rows // 8)
+    def _(group):
+        at = pl.ds(pl.multiple_of(group * 8, 8), 8)
+        for held, ref in ((th_s, th_ref), (w_s, w_ref)):
+            held[pl.ds(group * 8 + 3, 8)] = jnp.swapaxes(ref[:, at, :], 0, 1)
+        for held, ref in ((u_s, u_ref), (v_s, v_ref)):
+            held[pl.ds(group * 8, 8)] = jnp.swapaxes(ref[:, at, :], 0, 1)
+
+    @pl.when(tile == 0)
+    def _():
+        below = jnp.swapaxes(south[...], 0, 1)
+        for held, _, _, _, field in pairs:
+            held[0:3] = below[field : field + 3]
+        v_before = below[6]
+        th_q = [th_s[row] for row in range(6)]
+        w_q = [w_s[row] for row in range(6)]
+        flow_s[0] = flux60(*th_q, v_before * (time_step / 60.0))
+        flow_s[1] = flux60(*w_q, (v_before + upper_of(v_before)) * (0.5 * time_step / 60.0))
+        flow_s[2] = v_before
+        carry_s[...] = jnp.zeros_like(carry_s)
+
+    @pl.when(tile > 0)
+    def _():
+        for held, _, low, _, _ in pairs:
+            held[0:3] = jnp.swapaxes(low[...], 0, 1)[5:8]
+
+    @pl.when(tile == tiles - 1)
+    def _():
+        above = jnp.swapaxes(north[...], 0, 1)
+        for held, _, _, _, field in pairs:
+            held[rows + 3 : rows + 6] = above[field : field + 3]
+
+    @pl.when(tile < tiles - 1)
+    def _():
+        for held, _, _, top, _ in pairs:
+            held[rows + 3 : rows + 6] = jnp.swapaxes(top[...], 0, 1)[0:3]
+
+    def along_x(field, before, after, speed, face):
+        line = jnp.concatenate([before, field, after], axis=1)
+        parts = [line[:, 126 + k : 126 + k + cols] for k in range(6)]
+        flow = flux60(*parts, speed)
+        return flow - jnp.concatenate([face, flow], axis=1)[:, 127 : 127 + cols]
+
+    def along_z(field, ups, speed, inverse):
+        low = lower_of(field)
+        flow = flux60(lower_of(low), low, field, *ups, speed)
+        return (flow - zero_below(flow)) * inverse
+
+    def row(j, _):
+        rim = rim_ref[j]
+        coef = [wide(coef_ref[k], cols) for k in range(6)]
+        theta, w, u, v = th_s[j + 3], w_s[j + 3], u_s[j], v_s[j]
+        theta_ups = [upper_of(theta)]
+        w_ups = [upper_of(w)]
+        for _ in range(2):
+            theta_ups.append(upper_of(theta_ups[-1]))
+            w_ups.append(upper_of(w_ups[-1]))
+
+        flow = flux60(*[th_s[j + 1 + k] for k in range(6)], v * (time_step / 60.0))
+        change = flow - flow_s[0]
+        flow_s[0] = flow
+        change += along_x(
+            theta, pltpu.roll(rim, 116, 1), rim, u * (time_step / 60.0), pltpu.roll(rim, 121, 1)
+        )
+        change += along_z(theta, theta_ups, w * coef[0], coef[1])
+        new_s[j] = theta - change
+
+        u_sum = (u + upper_of(u)) * (0.5 * time_step / 60.0)
+        v_sum = (v + upper_of(v)) * (0.5 * time_step / 60.0)
+        flow = flux60(*[w_s[j + 1 + k] for k in range(6)], v_sum)
+        change = flow - flow_s[1]
+        flow_s[1] = flow
+        change += along_x(w, pltpu.roll(rim, 113, 1), pltpu.roll(rim, 125, 1), u_sum, pltpu.roll(rim, 120, 1))
+        change += along_z(w, w_ups, (w + w_ups[0]) * coef[2], coef[3])
+        star = w - change + (0.5 * time_step * buoyancy_gain) * (theta + theta_ups[0])
+        star_out[row_of(j, levels), :] = star
+
+        mass = coef[4] * star
+        u_west = jnp.concatenate([pltpu.roll(rim, 119, 1), u], axis=1)[:, 127 : 127 + cols]
+        source = (u - u_west + (v - flow_s[2])) * (1.0 / time_step) + (mass - zero_below(mass)) * coef[5]
+        flow_s[2] = v
+        modes_s[row_of(j, levels), :] = mix_levels(source, [wide(mixer_ref[k], cols) for k in range(levels)])
+        return 0
+
+    lax.fori_loop(0, rows, row, 0)
+
+    @pl.loop(0, rows // 8)
+    def _(group):
+        at = pl.ds(pl.multiple_of(group * 8, 8), 8)
+        theta_out[:, at, :] = jnp.swapaxes(new_s[pl.ds(group * 8, 8)], 0, 1)
+
+    total = rows * levels
+    spectral_out[...] = jnp.dot(modes_s[...], sine_ref[...], precision=high)
+    here = pl.ds(pl.multiple_of(tile * total, total), total)
+    edge_out[here, :] = spectral_out[:, 0:128]
+    decay = decay_ref[...]
+    carry_s[...] = forward_rows(
+        lambda j: spectral_out[row_of(j, levels), :], decay, work_s, tile * rows, rows, carry_s[...]
+    )
+
+    @pl.when(tile == tiles - 1)
+    def _():
+        backward_rows(carry_s[...], decay, start_ref[...], work_s, ends_out, rows * tiles)
+
+        @pl.loop(0, tiles)
+        def _(step):
+            at = pl.ds(pl.multiple_of(step * total, total), total)
+            lane = lax.broadcasted_iota(jnp.int32, (total, 128), 1)
+            near = jnp.where(lane == 0, edge_out[at, :], 0.0)
+            edge_out[at, :] = near - jnp.dot(work_s[at, :], weight_ref[...], precision=high)
+
+
+def advect(u_face, v_face, w_face, theta_field, sides, coef, mixer, tables):
+    levels, rows, cols = theta_field.shape
+    step = min(32, rows)
+    tiles = rows // step
+    south, north, rim = sides
+    sine, weight, decay, start = tables
+    block = pl.BlockSpec((levels, step, cols), lambda i: (0, i, 0))
+    low = pl.BlockSpec((levels, 8, cols), lambda i: (0, jnp.maximum(i * (step // 8) - 1, 0), 0))
+    top = pl.BlockSpec((levels, 8, cols), lambda i: (0, jnp.minimum((i + 1) * (step // 8), rows // 8 - 1), 0))
+
+    def whole(value):
+        return pl.BlockSpec(value.shape, lambda i: (0,) * value.ndim)
+
+    flat = pl.BlockSpec((step * levels, cols), lambda i: (i, 0))
+    big = jax.ShapeDtypeStruct((rows * levels, cols), jnp.float32)
+    edge = jax.ShapeDtypeStruct((rows * levels, 128), jnp.float32)
+    ends = jax.ShapeDtypeStruct((2, levels, cols), jnp.float32)
+
+    def held(count):
+        return pltpu.VMEM((count, levels, cols), jnp.float32)
+
+    return pl.pallas_call(
+        advect_kernel,
+        grid=(tiles,),
+        in_specs=[
+            block, low, top, block, low, top, block, block, whole(south), whole(north),
+            pl.BlockSpec((step, levels, 128), lambda i: (i, 0, 0)),
+            whole(coef), whole(mixer), whole(sine), whole(weight), whole(decay), whole(start),
+        ],
+        out_specs=(block, flat, flat, whole(edge), whole(ends)),
+        out_shape=(jax.ShapeDtypeStruct(theta_field.shape, jnp.float32), big, big, edge, ends),
+        scratch_shapes=[
+            held(step + 6), held(step + 6), held(step), held(step), held(step),
+            pltpu.VMEM((step * levels, cols), jnp.float32),
+            held(3),
+            pltpu.VMEM((levels, cols), jnp.float32),
+            pltpu.VMEM((rows * levels, cols), jnp.float32),
+        ],
+        compiler_params=pltpu.CompilerParams(vmem_limit_bytes=vmem_bytes),
+        name="advect",
+    )(
+        theta_field, theta_field, theta_field, w_face, w_face, w_face, u_face, v_face, south, north, rim,
+        coef, mixer, sine, weight, decay, start,
+    )
+
+
+def finish_kernel(
+    free_ref, next_ref, line_ref, line_next, ends_ref, up_ref, down_ref, decay_ref, sine_ref, mixer_ref, coef_ref,
+    star_ref, u_ref, v_ref, u_out, v_out, w_out, p_out, work_s, p_s, gx_s, gy_s, w_s,
+):
+    tile, tiles = pl.program_id(0), pl.num_programs(0)
+    levels, rows, cols = u_ref.shape
+    total = rows * levels
+    decay = decay_ref[...]
+    work_s[0:total, :] = free_ref[...]
+    work_s[total : total + levels, :] = jnp.where(
+        tile == tiles - 1, decay * free_ref[total - levels : total, :], next_ref[...]
+    )
+
+    def upward(j, carry):
+        value = decay * carry
+        work_s[row_of(j, levels), :] += value
+        return value
+
+    lax.fori_loop(0, rows + 1, upward, ends_ref[0] * up_ref[0], unroll=4)
+
+    def downward(j, carry):
+        work_s[row_of(rows - j, levels), :] += carry
+        return decay * carry
+
+    lax.fori_loop(0, rows + 1, downward, ends_ref[1] * down_ref[0], unroll=4)
+
+    lane = lax.broadcasted_iota(jnp.int32, (total, 128), 1)
+    work_s[0:total, 0:128] = jnp.where(lane == 0, line_ref[...], work_s[0:total, 0:128])
+    work_s[total : total + levels, 0:128] = jnp.where(
+        lane[:levels] == 0, line_next[...], work_s[total : total + levels, 0:128]
+    )
+    p_s[:, 0:cols] = jnp.dot(work_s[...], sine_ref[...], precision=high)
+    mixer = [mixer_ref[k] for k in range(levels)]
+    broad = [wide(tile_, cols) for tile_ in mixer]
+
+    def physical(j, _):
+        at = row_of(j, levels)
+        p_s[at, 0:cols] = mix_levels(p_s[at, 0:cols], broad)
+        return 0
+
+    lax.fori_loop(0, rows + 1, physical, 0)
+    spacing = wide(coef_ref[...], cols)
+    top = lax.broadcasted_iota(jnp.int32, (levels, cols), 0) == levels - 1
+
+    def gradient(j, _):
+        at = row_of(j, levels)
+        here = p_s[at, 0:cols]
+        beside = mix_levels(pltpu.roll(line_ref[at, :], 127, 1), mixer)
+        line = jnp.concatenate([here, beside], axis=1)
+        gx_s[j] = time_step * (line[:, 1 : cols + 1] - here)
+        gy_s[j] = time_step * (p_s[row_of(j + 1, levels), 0:cols] - here)
+        above = jnp.where(top, 0.0, pltpu.roll(here, levels - 1, 0))
+        w_s[j] = star_ref[at, :] - spacing * (above - here)
+        return 0
+
+    lax.fori_loop(0, rows, gradient, 0)
+
+    @pl.loop(0, rows // 8)
+    def _(group):
+        at = pl.ds(pl.multiple_of(group * 8, 8), 8)
+        some = pl.ds(group * 8, 8)
+        u_out[:, at, :] = u_ref[:, at, :] - jnp.swapaxes(gx_s[some], 0, 1)
+        v_out[:, at, :] = v_ref[:, at, :] - jnp.swapaxes(gy_s[some], 0, 1)
+        w_out[:, at, :] = jnp.swapaxes(w_s[some], 0, 1)
+        flat = pl.ds(pl.multiple_of(group * 8 * levels, 8 * levels), 8 * levels)
+        p_out[:, at, :] = jnp.swapaxes(p_s[flat, 0:cols].reshape(8, levels, cols), 0, 1)
+
+
+def finish(free, lines, ends, decay, sine, mixer, spacing, star, u_face, v_face):
+    levels, rows, cols = u_face.shape
+    step = min(32, rows)
+    tiles = rows // step
+    hop = power(decay, step)
+    powers = [jnp.ones_like(decay)]
+    for _ in range(tiles - 1):
+        powers.append(powers[-1] * hop)
+    powers = jnp.stack(powers)
+    block = pl.BlockSpec((levels, step, cols), lambda i: (0, i, 0))
+    flat = pl.BlockSpec((step * levels, cols), lambda i: (i, 0))
+    ahead = pl.BlockSpec((levels, cols), lambda i: (jnp.minimum((i + 1) * step, rows - 1), 0))
+
+    def whole(value):
+        return pl.BlockSpec(value.shape, lambda i: (0,) * value.ndim)
+
+    out = jax.ShapeDtypeStruct(u_face.shape, jnp.float32)
+
+    def held(count):
+        return pltpu.VMEM((count, levels, cols), jnp.float32)
+
+    return pl.pallas_call(
+        finish_kernel,
+        grid=(tiles,),
+        in_specs=[
+            flat, ahead,
+            pl.BlockSpec((step * levels, 128), lambda i: (i, 0)),
+            pl.BlockSpec((levels, 128), lambda i: ((i + 1) * step, 0)),
+            whole(ends),
+            pl.BlockSpec((1, levels, cols), lambda i: (i, 0, 0)),
+            pl.BlockSpec((1, levels, cols), lambda i: (tiles - 1 - i, 0, 0)),
+            whole(decay), whole(sine), whole(mixer), whole(spacing), flat, block, block,
+        ],
+        out_specs=(block,) * 4,
+        out_shape=(out,) * 4,
+        scratch_shapes=[
+            pltpu.VMEM(((step + 1) * levels, cols), jnp.float32),
+            pltpu.VMEM(((step + 1) * levels, cols), jnp.float32),
+            held(step), held(step), held(step),
+        ],
+        compiler_params=pltpu.CompilerParams(vmem_limit_bytes=vmem_bytes),
+        name="finish",
+    )(free, free, lines, lines, ends, powers, powers, decay, sine, mixer, spacing, star, u_face, v_face)
+
+
+def tile_of(values):
+    return jnp.broadcast_to(values[..., None], values.shape + (128,))
+
+
+def rolled_mixer(matrix):
+    levels = matrix.shape[0]
+    index = np.arange(levels)
+    return tile_of(jnp.stack([matrix[index, (index - shift) % levels] for shift in range(levels)]))
+
+
+def per_device(u_face, v_face, w_face, theta_field, density, thickness):
+    levels, rows, cols = theta_field.shape
+    north, south, east, west = pack_sides(u_face, v_face, w_face, theta_field)
+    south_halo, north_halo = from_behind(north, "gy", 1), from_behind(south, "gy", -1)
+    west_halo, east_halo = from_behind(east, "gx", 1), from_behind(west, "gx", -1)
+
+    face_density = (density + lift_level(density)) / 2.0
+    face_spacing = (thickness + lift_level(thickness)) / 2.0
+    forward, back, square = vertical_modes(density, thickness, face_density, face_spacing)
+    mass = density * thickness
+    coef = tile_of(
+        jnp.stack(
+            [
+                face_density / 60.0,
+                time_step / mass,
+                lift_level(density) / 120.0,
+                time_step / (face_density * face_spacing),
+                face_density,
+                1.0 / (mass * time_step),
+            ]
+        )
+    )
+    index = np.arange(cols)
+    excess = (4.0 * np.sin(np.pi * index / (2 * cols)) ** 2).astype(np.float32) + square[:, None]
     decay = jnp.where(index[None, :] > 0, decay_of(excess), 0.0)
     start = -1.0 / (1.0 - decay * decay)
     ratio = power(decay, rows)
-    big = jax.ShapeDtypeStruct((total, cols_x), jnp.float32)
-    strip = jax.ShapeDtypeStruct((total, 128), jnp.float32)
-    ends = jax.ShapeDtypeStruct((2, levels, cols_x), jnp.float32)
-    scratch = [pltpu.VMEM((total, cols_x), jnp.float32)]
+    sine = sine_matrix(cols)
+    weight = edge_weights(cols)
+
+    sides = (south_halo, north_halo, rim_lanes(west_halo, east_halo, west))
+    theta_new, star, spectral, edge, free_ends = advect(
+        u_face, v_face, w_face, theta_field, sides, coef, rolled_mixer(forward), (sine, weight, decay, start)
+    )
+    big = jax.ShapeDtypeStruct(spectral.shape, jnp.float32)
+    scratch = [pltpu.VMEM(spectral.shape, jnp.float32)]
     params = pltpu.CompilerParams(vmem_limit_bytes=vmem_bytes)
-
-    def call(kernel, outs, name):
-        return pl.pallas_call(kernel, out_shape=outs, scratch_shapes=scratch, compiler_params=params, name=name)
-
-    spectral, edge, free_ends = call(first_kernel, (big, strip, ends), "first_solve")(
-        modes, sine, weight, decay, start
-    )
-    edge = call(second_kernel, strip, "edge_terms")(decay, couple(free_ends, ratio), weight, edge)
-    lines = separator_solve(edge, square, rows, cols_x)
-    free, free_ends = call(third_kernel, (big, ends), "second_solve")(
-        spectral, lines, weight.T, decay, start
-    )
-    return call(fourth_kernel, big, "to_columns")(free, lines, sine, decay, couple(free_ends, ratio))
-
-
-def shift_gradient(pressure):
-    east_cells = from_behind(pressure[:, :, :1], "gx", -1)
-    north_cells = from_behind(pressure[:, :1, :], "gy", -1)
-    grad_x = jnp.concatenate([pressure[:, :, 1:], east_cells], axis=2) - pressure
-    grad_y = jnp.concatenate([pressure[:, 1:, :], north_cells], axis=1) - pressure
-    return (grad_x, grad_y)
-
-
-def per_device(u_face, v_face, w_face, theta_field, density, thickness):
-    levels, rows_y, cols_x = theta_field.shape
-    theta_rim, w_rim, u_rim, v_rim = (
-        extended(theta_field, (("gx", 2), ("gy", 1)), 3),
-        extended(w_face, (("gx", 2), ("gy", 1)), 3),
-        extended(u_face, (("gx", 2), ("gy", 1)), 3),
-        extended(v_face, (("gx", 2), ("gy", 1)), 3),
-    )
-    face_density = (density + lift_level(density)) / 2.0
-    face_spacing = (thickness + lift_level(thickness)) / 2.0
-    forward, back, square = vertical_modes(density, thickness, face_density, face_spacing)
-    adv_theta = horizontal_local(theta_rim, u_rim, v_rim, rows_y, cols_x) + vertical_tend(
-        theta_field, w_face, face_density, density, thickness
-    )
-    u_level = (u_rim + lift_level(u_rim)) / 2.0
-    v_level = (v_rim + lift_level(v_rim)) / 2.0
-    w_level = (w_face + lift_level(w_face)) / 2.0
-    adv_w = horizontal_local(w_rim, u_level, v_level, rows_y, cols_x) + vertical_tend(
-        w_face, w_level, lift_level(density), face_density, face_spacing
-    )
-    theta_new = theta_field + time_step * adv_theta
-    w_star = w_face + time_step * (
-        adv_w + buoyancy_gain * (theta_field + lift_level(theta_field)) / 2.0
-    )
-    mass_flux = face_density[:, None, None] * w_star
-    mass_below = jnp.concatenate([jnp.zeros_like(mass_flux[:1]), mass_flux[:-1]], axis=0)
-    divergence = (
-        u_face
-        - u_rim[:, 3 : 3 + rows_y, 2 : 2 + cols_x]
-        + (v_face - v_rim[:, 2 : 2 + rows_y, 3 : 3 + cols_x])
-    )
-    divergence = divergence + (mass_flux - mass_below) / (density * thickness)[:, None, None]
-    source_term = divergence / time_step
-    modes = jnp.einsum("kl,lyx->ykx", forward, source_term, precision=high)
-    solved = pressure_modes(modes.reshape(rows_y * levels, cols_x), square)
-    pressure = jnp.einsum("kl,ykx->lyx", back, solved.reshape(rows_y, levels, cols_x), precision=high)
-    grad_x, grad_y = shift_gradient(pressure)
-    u_new = u_face - time_step * grad_x
-    v_new = v_face - time_step * grad_y
-    above = jnp.concatenate([pressure[1:], jnp.zeros_like(pressure[:1])], axis=0)
-    w_new = w_star - time_step * (above - pressure) / face_spacing[:, None, None]
+    edge = pl.pallas_call(
+        second_kernel,
+        out_shape=jax.ShapeDtypeStruct(edge.shape, jnp.float32),
+        scratch_shapes=scratch,
+        compiler_params=params,
+        name="edge_terms",
+    )(decay, couple(free_ends, ratio), weight, edge)
+    lines = separator_solve(edge, square, rows, cols)
+    free, free_ends = pl.pallas_call(
+        third_kernel,
+        out_shape=(big, jax.ShapeDtypeStruct(free_ends.shape, jnp.float32)),
+        scratch_shapes=scratch,
+        compiler_params=params,
+        name="second_solve",
+    )(spectral, lines[: rows * levels], weight.T, decay, start)
+    u_new, v_new, w_new, pressure = finish(
+        free, lines, couple(free_ends, ratio), decay, sine, rolled_mixer(back.T),
+        tile_of(time_step / face_spacing), star, u_face, v_face,
+    )
     return (u_new, v_new, w_new, theta_new, pressure)
 
 

time: 457 us -> 355 us (0.78)
  other arithmetic: 179 us -> 11.3 us
  Pallas kernels: 53.8 us -> 208 us
  local copies, waits for them, and re-layouts: 96.5 us -> 46.3 us
  starting transfers between devices: 27 us -> 7.55 us
  matrix products: 26.5 us -> 8.76 us
    pallas_call x4 -> x5, Pallas kernels: 49.4 us -> 204 us  [the longest x1 120 us: advect(): pl.pallas_call(advect_kernel, grid=(tiles,), in_specs=[block, low, top, b...]
    sub x5 -> x1, other arithmetic: 90.9 us -> 6.57 us  [flux60(): return speed * centred - jnp.abs(speed) * damped]
    mul x3 -> x0, other arithmetic: 48.6 us -> none  [the longest x1 30.3 us: per_device(): mass_flux = face_density[:, None, None] * w_star]
    unnamed x173 -> x61, local copies, waits for them, and re-layouts: 48.2 us -> 3 us
    concatenate x6 -> x1, other arithmetic: 26.5 us -> 0.01 us  [rolled_mixer(): matrix[index, (index - shift) % levels]]
    ppermute x16 -> x0, starting transfers between devices: 26.3 us -> none  [the longest x8 18.6 us: extended(): after = lax.ppermute(first, axis, down)]
    dot_general x2 -> x0, matrix products: 19.4 us -> none  [the longest x1 13.6 us: per_device(): modes = jnp.einsum('kl,lyx->ykx', forward, source_term, precision=high)]
    ppermute x9 -> x0, local copies, waits for them, and re-layouts: 10.2 us -> none  [the longest x4 5.29 us: extended(): after = lax.ppermute(first, axis, down)]
  transfers between devices with their start and end apart: 18 -> 4, of which waited for: 0 -> 0; matrix products, arithmetic and copies ran while one was open for 39% -> 14% of each run, Pallas kernels for 1% -> 1%
where the time goes in v2:
time: 355 us; the launch traced here: 354 us
  Pallas kernels  208 us (59%)
  blocking collectives  70.5 us (20%)
  local copies, waits for them, and re-layouts  46.3 us (13%)
  other arithmetic  11.3 us (3%)
  matrix products  8.76 us (2%)
  starting transfers between devices  7.55 us (2%)
    pallas_call x1, Pallas kernels, advect(): pl.pallas_call(advect_kernel, grid=(tiles,), in_specs=[block, low, top, b...  120 us
    pallas_call x1, Pallas kernels, finish(): pl.pallas_call(finish_kernel, grid=(tiles,), in_specs=[flat, ahead, pl.Bl...  61 us
    all_gather x1, blocking collectives, separator_solve(): lines = lax.all_gather(sides, ('gx', 'gy'))  41.9 us
    all_gather x2, blocking collectives, couple(): gathered = lax.all_gather(ends, 'gy')  28.6 us
    gather x16, local copies, waits for them, and re-layouts, rolled_mixer(): matrix[index, (index - shift) % levels]  10.2 us
    pallas_call x1, Pallas kernels, per_device(): pl.pallas_call(third_kernel, out_shape=(big, jax.ShapeDtypeStruct(free_en...  8.66 us
    slice x7, local copies, waits for them, and re-layouts, rim_lanes(): west[:, f]  8.18 us
    ppermute x4, starting transfers between devices, from_behind(): return lax.ppermute(value, axis, pairs)  7.55 us
  transfers between devices with their start and end apart: 4, of which 0 were waited for; matrix products, arithmetic and copies ran while one was open for 14% of the time, Pallas kernels for 1%

profile of v2, /device:TPU:0, one launch (start us, length us, event | category | flops | bytes accessed | tf_op | source)
XLA Modules:
  0.0 354.2 jit_solution(7300720218979918324)
XLA Ops:
  0.7 7.2 %pack_sides.1 = (f32[8,8,512]{2,1,0:T(8,128)}, f32[8,8,512]{2,1,0:T(8,128)}, f32[8,8,256]{2,1,0:T(8,128)}, f32[8,8,256]{2,1,0:T(8,128)}) custom-call(f32[8,256,512]{2,1,0:T(8,128)} %th_hi.3, f32[8,256,512]{2,1,0:T(8,128)} %th_hi.3, f32[8,256,512]{2,1,0:T(8,128)} %w_hi.3, f32[8,256,512]{2,1,0:T(8,128)} %w_hi.3, f32[8,256,512]{2,1,0:T(8,128)} %v_ref.3, ...), custom_call_target="tpu_custom_call" | custom-call | tf_op jit(solution)/shard_map/pack_sides/pallas_call | solution.py:338
  7.9 3.0 collective-permute-start.3
  12.0 3.5 collective-permute-start.1
  20.4 4.4 %vertical_modes.1 = (f32[8,8,128]{2,1,0:T(8,128)}, f32[8,8,128]{2,1,0:T(8,128)}) custom-call(f32[8,8,128]{2,1,0:T(8,128)} %broadcast_in_dim.235.columns_ref), custom_call_target="tpu_custom_call" | custom-call | tf_op jit(solution)/shard_map/vertical_modes/pallas_call | solution.py:88
  38.1 1.3 copy.205
  39.4 1.3 copy.203
  40.8 1.3 copy.191
  42.1 1.4 copy.189
  43.5 1.4 copy.187
  45.9 1.3 copy.200
  47.2 1.3 copy.198
  49.0 1.3 copy.204
  50.4 1.3 copy.202
  51.7 1.4 copy.190
  53.1 1.4 copy.188
  54.5 1.3 copy.186
  55.8 6.6 %multiply_subtract_fusion = (f32[8,1,256]{1,0,2:T(8,128)}, f32[8,1,256]{1,0,2:T(8,128)}) fusion(f32[8,1,256]{1,0,2:T(8,128)} %copy.205, f32[8,1,256]{1,0,2:T(8,128)} %copy.204, f32[8,1,256]{1,0,2:T(8,128)} %copy.203, f32[8,1,256]{1,0,2:T(8,128)} %copy.202, f32[8,1,256]{1,0,2:T(8,128)S(1)} %copy.201, f32[8,1,256]{1,0,2:T(8,128)} %copy.200, ...), kind=kLoop, calls=%fused_computation.29 | loop fusion | flops 81920 | bytes 131072 | tf_op jit(solution)/shard_map/sub | solution.py:303
  62.4 1.3 copy.212
  63.7 1.3 copy.213
  65.1 4.6 %concatenate.91 = f32[8,15,256]{1,0,2:T(8,128)} concatenate(f32[8,6,256]{1,0,2:T(8,128)} %copy.212, f32[8,1,256]{1,0,2:T(8,128)} %get-tuple-element.50, f32[8,1,256]{1,0,2:T(8,128)} %get-tuple-element.49, f32[8,1,256]{1,0,2:T(8,128)S(1)} %copy.227, f32[8,6,256]{1,0,2:T(8,128)} %copy.213), dimensions={1} | concatenate | bytes 245760 | tf_op jit(solution)/shard_map/concatenate | solution.py:352
  69.7 1.3 pad.8.rim_ref
  71.2 119.9 %advect.1 = (f32[8,256,512]{2,1,0:T(8,128)}, f32[2048,512]{1,0:T(8,128)}, f32[2048,512]{1,0:T(8,128)}, f32[2048,128]{1,0:T(8,128)S(1)}, f32[2,8,512]{2,1,0:T(8,128)S(1)}) custom-call(f32[8,256,512]{2,1,0:T(8,128)} %th_hi.3, f32[8,256,512]{2,1,0:T(8,128)} %th_hi.3, f32[8,256,512]{2,1,0:T(8,128)} %th_hi.3, f32[8,256,512]{2,1,0:T(8,128)} %w_hi.3, ...), custom_call_target="tpu_custom_call" | custom-call | tf_op jit(solution)/shard_map/advect/pallas_call | solution.py:501
  191.1 14.4 %all-gather = f32[16,8,512]{2,1,0:T(8,128)S(1)} all-gather(f32[2,8,512]{2,1,0:T(8,128)S(1)} %get-tuple-element.29), channel_id=2, replica_groups=mesh['gx'=4,'gy'=8] {'gy'}, dimensions={0}, use_global_device_ids=true | all-gather | bytes 294912 | tf_op jit(solution)/shard_map/all_gather | solution.py:196
  205.7 7.1 %edge_terms.1 = f32[2048,128]{1,0:T(8,128)S(1)} custom-call(f32[8,512]{1,0:T(8,128)S(1)} %get-tuple-element.77.decay_ref, f32[2,8,512]{2,1,0:T(8,128)S(1)} %pad_maximum_fusion.2.ends_ref, f32[512,128]{1,0:T(8,128)S(1)} %copy-done.2, f32[2048,128]{1,0:T(8,128)S(1)} %get-tuple-element.30.edge_in_ref), custom_call_target="tpu_custom_call" | custom-call | tf_op jit(solution)/shard_map/edge_terms/pallas_call | solution.py:686
  213.2 41.9 %all-gather.1 = f32[64,8,256]{2,1,0:T(8,128)S(1)} all-gather(f32[2,8,256]{2,1,0:T(8,128)S(1)} %bitcast.138), channel_id=3, replica_groups=mesh['gx'=4,'gy'=8] {'gx','gy'}, dimensions={0}, use_global_device_ids=true | all-gather | bytes 540672 | tf_op jit(solution)/shard_map/all_gather | solution.py:257
  255.7 1.2 squeeze.15
  256.9 3.0 fusion
  260.0 3.0 convolution_bitcast_fusion
  267.8 8.7 %second_solve.1 = (f32[2048,512]{1,0:T(8,128)S(1)}, f32[2,8,512]{2,1,0:T(8,128)S(1)}) custom-call(f32[2048,512]{1,0:T(8,128)} %get-tuple-element.28.spectral_ref, f32[2048,128]{1,0:T(8,128)S(1)} %pad_slice_fusion.line_ref, f32[128,512]{1,0:T(8,128)S(1)} %copy-done.3, f32[8,512]{1,0:T(8,128)S(1)} %get-tuple-element.77.decay_ref, ...), custom_call_target="tpu_custom_call" | custom-call | tf_op jit(solution)/shard_map/second_solve/pallas_call | solution.py:694
  276.5 2.0 copy-done
  278.5 14.2 %all-gather.2 = f32[16,8,512]{2,1,0:T(8,128)S(1)} all-gather(f32[2,8,512]{2,1,0:T(8,128)S(1)} %get-tuple-element.32), channel_id=4, replica_groups=mesh['gx'=4,'gy'=8] {'gy'}, dimensions={0}, use_global_device_ids=true | all-gather | bytes 294912 | tf_op jit(solution)/shard_map/all_gather | solution.py:196
  293.2 61.0 %finish.1 = (f32[8,256,512]{2,1,0:T(8,128)}, f32[8,256,512]{2,1,0:T(8,128)}, f32[8,256,512]{2,1,0:T(8,128)}, f32[8,256,512]{2,1,0:T(8,128)}) custom-call(f32[2048,512]{1,0:T(8,128)} %copy-done, f32[2048,512]{1,0:T(8,128)} %copy-done, f32[2056,128]{1,0:T(8,128)S(1)} %pad.9.line_ref.line_next, f32[2056,128]{1,0:T(8,128)S(1)} %pad.9.line_ref.line_next, ...), custom_call_target="tpu_custom_call" | custom-call | tf_op jit(solution)/shard_map/finish/pallas_call | solution.py:615
  (152 shorter events, 26.7 us)
Async XLA Ops:
  0.6 19.1 %copy-start.25 = (f32[8,8]{0,1:T(8,128)S(1)}, f32[8,8]{0,1:T(8,128)}, u32[]{:S(2)}) copy-start(f32[8,8]{0,1:T(8,128)} %constant.158.clone) | copy-start | bytes 772
  0.6 19.1 %copy-start.26 = (f32[8,8]{0,1:T(8,128)S(1)}, f32[8,8]{0,1:T(8,128)}, u32[]{:S(2)}) copy-start(f32[8,8]{0,1:T(8,128)} %constant.157.clone) | copy-start | bytes 772
  0.7 25.0 %copy-start.13 = (s32[8]{0:T(128)S(1)}, s32[8]{0:T(128)}, u32[]{:S(2)}) copy-start(s32[8]{0:T(128)} %constant.465) | copy-start | bytes 100
  0.7 27.6 %copy-start.12 = (s32[8]{0:T(128)S(1)}, s32[8]{0:T(128)}, u32[]{:S(2)}) copy-start(s32[8]{0:T(128)} %constant.457) | copy-start | bytes 100
  0.7 28.9 %copy-start.11 = (s32[8]{0:T(128)S(1)}, s32[8]{0:T(128)}, u32[]{:S(2)}) copy-start(s32[8]{0:T(128)} %constant.449) | copy-start | bytes 100
  0.7 14.8 %copy-start.28 = (f32[8]{0:T(128)S(1)}, f32[8]{0:T(128)}, u32[]{:S(2)}) copy-start(f32[8]{0:T(128)} %param.81) | copy-start | bytes 100
  0.7 15.5 %copy-start.27 = (f32[8]{0:T(128)S(1)}, f32[8]{0:T(128)}, u32[]{:S(2)}) copy-start(f32[8]{0:T(128)} %param.80) | copy-start | bytes 100
  7.9 22.9 %copy-start.10 = (s32[8]{0:T(128)S(1)}, s32[8]{0:T(128)}, u32[]{:S(2)}) copy-start(s32[8]{0:T(128)} %constant.441) | copy-start | bytes 100
  7.9 24.2 %copy-start.9 = (s32[8]{0:T(128)S(1)}, s32[8]{0:T(128)}, u32[]{:S(2)}) copy-start(s32[8]{0:T(128)} %constant.433) | copy-start | bytes 100
  7.9 25.5 %copy-start.8 = (s32[8]{0:T(128)S(1)}, s32[8]{0:T(128)}, u32[]{:S(2)}) copy-start(s32[8]{0:T(128)} %constant.425) | copy-start | bytes 100
  7.9 26.7 %copy-start.7 = (s32[8]{0:T(128)S(1)}, s32[8]{0:T(128)}, u32[]{:S(2)}) copy-start(s32[8]{0:T(128)} %constant.417) | copy-start | bytes 100
  7.9 37.7 %collective-permute-start.3 = (f32[8,8,256]{2,1,0:T(8,128)}, f32[8,8,256]{2,1,0:T(8,128)S(1)}, u32[]{:S(2)}, u32[]{:S(2)}) collective-permute-start(f32[8,8,256]{2,1,0:T(8,128)} %get-tuple-element.25), channel_id=1, source_target_pairs={{0,8},{8,16},{16,24},{24,0},{1,9},{9,17},{17,25},{25,1},{2,10},{10... | collective-permute-start | bytes 196616 | tf_op jit(solution)/shard_map/ppermute | solution.py:18
  10.9 51.4 %collective-permute-start.2 = (f32[8,8,256]{2,1,0:T(8,128)}, f32[8,8,256]{2,1,0:T(8,128)S(1)}, u32[]{:S(2)}, u32[]{:S(2)}) collective-permute-start(f32[8,8,256]{2,1,0:T(8,128)} %get-tuple-element.24), channel_id=1, source_target_pairs={{0,24},{8,0},{16,8},{24,16},{1,25},{9,1},{17,9},{25,17},{2,26},{10... | collective-permute-start | bytes 196616 | tf_op jit(solution)/shard_map/ppermute | solution.py:18
  12.0 59.0 %collective-permute-start = (f32[8,8,512]{2,1,0:T(8,128)}, f32[8,8,512]{2,1,0:T(8,128)S(1)}, u32[]{:S(2)}, u32[]{:S(2)}) collective-permute-start(f32[8,8,512]{2,1,0:T(8,128)} %get-tuple-element.22), channel_id=1, source_target_pairs={{0,1},{1,2},{2,3},{3,4},{4,5},{5,6},{6,7},{7,0},{8,9},{9,10},{10,1... | collective-permute-start | bytes 393224 | tf_op jit(solution)/shard_map/ppermute | solution.py:18
  12.0 59.0 %collective-permute-start.1 = (f32[8,8,512]{2,1,0:T(8,128)}, f32[8,8,512]{2,1,0:T(8,128)S(1)}, u32[]{:S(2)}, u32[]{:S(2)}) collective-permute-start(f32[8,8,512]{2,1,0:T(8,128)} %get-tuple-element.23), channel_id=1, source_target_pairs={{0,7},{1,0},{2,1},{3,2},{4,3},{5,4},{6,5},{7,6},{8,15},{9,8},{10,9... | collective-permute-start | bytes 393224 | tf_op jit(solution)/shard_map/ppermute | solution.py:18
  25.7 10.2 %copy-start.15 = (f32[8,8,256]{2,1,0:T(8,128)S(1)}, f32[8,8,256]{2,1,0:T(8,128)}, u32[]{:S(2)}) copy-start(f32[8,8,256]{2,1,0:T(8,128)} %get-tuple-element.24) | copy-start | bytes 196612
  25.7 11.2 %copy-start.6 = (f32[512]{0:T(512)S(1)}, f32[512]{0:T(512)}, u32[]{:S(2)}) copy-start(f32[512]{0:T(512)} %constant.159.clone) | copy-start | bytes 6148
  25.7 11.2 %copy-start.14 = (pred[512]{0:T(512)(128)(4,1)S(1)}, pred[512]{0:T(512)(128)(4,1)}, u32[]{:S(2)}) copy-start(pred[512]{0:T(512)(128)(4,1)} %constant.201) | copy-start | bytes 1540
  65.1 6.1 %copy-start.1 = (f32[512,512]{1,0:T(8,128)S(1)}, f32[512,512]{1,0:T(8,128)}, u32[]{:S(2)}) copy-start(f32[512,512]{1,0:T(8,128)} %constant.169.clone.sine_ref) | copy-start | bytes 3145732
  65.1 6.1 %copy-start.2 = (f32[512,128]{1,0:T(8,128)S(1)}, f32[512,128]{1,0:T(8,128)}, u32[]{:S(2)}) copy-start(f32[512,128]{1,0:T(8,128)} %constant.170.clone.weight_ref) | copy-start | bytes 786436
  205.7 51.2 %copy-start.19 = (f32[64,64,1]{1,0,2:T(8,128)S(1)}, f32[64,64,1]{1,0,2:T(8,128)}, u32[]{:S(2)}) copy-start(f32[64,64,1]{1,0,2:T(8,128)} %constant.523) | copy-start | bytes 49156
  213.2 46.7 %copy-start.18 = (f32[64,64,1]{1,0,2:T(8,128)S(1)}, f32[64,64,1]{1,0,2:T(8,128)}, u32[]{:S(2)}) copy-start(f32[64,64,1]{1,0,2:T(8,128)} %constant.522) | copy-start | bytes 49156
  255.4 7.7 %copy-start.4 = (f32[64,32]{0,1:T(8,128)S(1)}, f32[64,32]{0,1:T(8,128)}, u32[]{:S(2)}) copy-start(f32[64,32]{0,1:T(8,128)} %constant.174.clone) | copy-start | bytes 24580
  255.4 7.7 %copy-start.5 = (f32[64,32]{0,1:T(8,128)S(1)}, f32[64,32]{0,1:T(8,128)}, u32[]{:S(2)}) copy-start(f32[64,32]{0,1:T(8,128)} %constant.173.clone) | copy-start | bytes 24580
  255.4 7.7 %copy-start.22 = (f32[32,32,1]{0,1,2:T(8,128)S(1)}, f32[32,32,1]{0,1,2:T(8,128)}, u32[]{:S(2)}) copy-start(f32[32,32,1]{0,1,2:T(8,128)} %constant.524) | copy-start | bytes 12292
  255.7 8.1 %copy-start.21 = (f32[32,32,1]{0,1,2:T(8,128)S(1)}, f32[32,32,1]{0,1,2:T(8,128)}, u32[]{:S(2)}) copy-start(f32[32,32,1]{0,1,2:T(8,128)} %constant.525) | copy-start | bytes 12292
  260.0 4.6 %copy-start.20 = (f32[64,32]{0,1:T(8,128)S(1)}, f32[64,32]{0,1:T(8,128)}, u32[]{:S(2)}) copy-start(f32[64,32]{0,1:T(8,128)} %constant.177.clone) | copy-start | bytes 24580
  260.0 5.0 %copy-start.24 = (f32[32,32,1]{0,1,2:T(8,128)S(1)}, f32[32,32,1]{0,1,2:T(8,128)}, u32[]{:S(2)}) copy-start(f32[32,32,1]{0,1,2:T(8,128)} %constant.527) | copy-start | bytes 12292
  263.1 2.3 copy-start.23
  263.1 2.7 copy-start.17
  263.1 3.0 copy-start.16
  276.5 2.0 copy-start
  (1 other events, 1.7 us)
